TPU v7x, 32 devices: a whole 2x2x4 slice. The times are simulated.
32 devices in a mesh: sky: 8 (over z, x), band: 4 (over y, core).
Axes of the slice: x: 2, y: 2, z: 4, core: 2. Of those that a mesh axis runs over, the one named last changes fastest.
Arguments:
- raw_blocks: bfloat16 [168, 172032], P(None, ('sky', 'band')), may hold values from -6 to 6
- patch_of_block: int32 [1024, 1], P(('sky', 'band')), may hold values from 0 to 7; in each aligned block of 32 rows (0 to 31, 32 to 63, ...) at most 8 rows name the same one
- cell_of_block: int32 [1024], P(('sky', 'band')), may hold values from 0 to 15
- band_of_block: int32 [1024], P(('sky', 'band')), may hold values from 0 to 5
- block_weight: bfloat16 [1024], P(('sky', 'band')), may hold values from 0.25 to 4
- basis_coef: bfloat16 [1024, 3], P(('sky', 'band')), may hold values from 0.25 to 1
- row_basis: float32 [3, 41], replicated, may hold values from -1 to 1
- col_basis: float32 [3, 41], replicated, may hold values from -1 to 1
- band_gain: float32 [6], replicated, may hold values from 0.5 to 2
- filter_taps: float32 [41], replicated, may hold values from -1 to 1
Outputs:
- detection: float32 [8, 512, 512], P('sky', 'band')
Inputs may be any that keep to these rules, and one draw needn't show every extreme that they name: `patch_of_block`: of the 32 blocks of one device at most 8 intersect one patch, and on some device exactly 8 do.
All inputs are finite; a program needn't handle non-finite values.
Results may differ from a plain program's by a relative error of at most 0.015.
Values may be sent and summed in bfloat16 or wider, within the bound.
No kernel may reach another device: no remote copies, remote signals or barrier semaphores. Data moves between devices by JAX's collectives and lax.ppermute only.
A program may use at most 128 MiB of HBM per device.

v0:
```python
import jax
import jax.numpy as jnp
from jax import lax
from jax.sharding import PartitionSpec as P

BANDS = 6
CR = 4
CC = 4
CELLS = 16


def extended(block, sides, width):
    for axis, dim in sides:
        count = lax.axis_size(axis)
        forward = [(i, i + 1) for i in range(count - 1)]
        backward = [(target, source) for source, target in forward]
        low = lax.ppermute(
            lax.slice_in_dim(block, block.shape[dim] - width, None, axis=dim), axis, forward
        )
        high = lax.ppermute(lax.slice_in_dim(block, 0, width, axis=dim), axis, backward)
        block = jnp.concatenate([low, block, high], axis=dim)
    return block


def toeplitz(tap_values, rows_out):
    tap_count = tap_values.shape[0]
    period = jnp.concatenate([tap_values, jnp.zeros((rows_out,), tap_values.dtype)])
    flat_row = jnp.tile(period, rows_out)[: rows_out * (rows_out + tap_count - 1)]
    return flat_row.reshape(rows_out, rows_out + tap_count - 1)


def kernel_stack(basis_taps, rows_out):
    return jnp.stack(
        [toeplitz(basis_taps[k], rows_out) for k in range(basis_taps.shape[0])]
    ).astype(jnp.bfloat16)


def match_one(row_kernels, col_kernels, raw_block, coefficient):
    sectioned = jnp.einsum(
        "kip,pq->kiq", row_kernels, raw_block, preferred_element_type=jnp.float32
    ).astype(jnp.bfloat16)
    basis_terms = jnp.einsum(
        "kiq,kjq->kij", sectioned, col_kernels, preferred_element_type=jnp.float32
    )
    return jnp.sum(coefficient.astype(jnp.float32)[:, None, None] * basis_terms, axis=0).astype(
        jnp.bfloat16
    )


def match_many(row_kernels, col_kernels, raw_many, coef_many):

    def single(block_pair):
        return match_one(row_kernels, col_kernels, block_pair[0], block_pair[1])

    return lax.map(single, (raw_many, coef_many), batch_size=16)


def local(
    raw_blocks,
    patch_of_block,
    cell_of_block,
    band_of_block,
    block_weight,
    basis_coef,
    row_basis,
    col_basis,
    band_gain,
    filter_taps,
):
    sky_count = lax.axis_size("sky")
    band_count = lax.axis_size("band")
    margin_side = raw_blocks.shape[0]
    block_count = raw_blocks.shape[1] // margin_side
    basis_count = row_basis.shape[0]
    radius = (filter_taps.shape[0] - 1) // 2
    block_side = margin_side - 2 * radius
    capacity = max(2, (2 * block_count + sky_count - 1) // sky_count)
    slot_count = sky_count * capacity
    row_kernels = kernel_stack(row_basis, block_side)
    col_kernels = kernel_stack(col_basis, block_side)
    block_major = raw_blocks.reshape(margin_side, block_count, margin_side).transpose(1, 0, 2)
    owner_patch = patch_of_block[:, 0]
    positions = jnp.arange(block_count, dtype=jnp.int32)
    earlier_peer = (owner_patch[:, None] == owner_patch[None, :]) & (
        positions[None, :] < positions[:, None]
    )
    rank_within = jnp.sum(earlier_peer.astype(jnp.int32), axis=1)
    slot_index = owner_patch * capacity + rank_within
    wanted = slot_index[None, :] == jnp.arange(slot_count, dtype=jnp.int32)[:, None]
    source = jnp.sum(jnp.where(wanted, positions[None, :], 0), axis=1) + jnp.where(
        jnp.any(wanted, axis=1), 0, block_count
    )
    details = jnp.concatenate(
        [
            block_weight[:, None],
            basis_coef,
            cell_of_block[:, None].astype(jnp.bfloat16),
            band_of_block[:, None].astype(jnp.bfloat16),
        ],
        axis=1,
    )
    detail_width = details.shape[1]
    outgoing_details = jnp.take(details, source, axis=0, mode="fill", fill_value=0).reshape(
        sky_count, capacity, detail_width
    )
    outgoing = jnp.take(block_major, source, axis=0, mode="fill", fill_value=0).reshape(
        sky_count, capacity, margin_side, margin_side
    )
    raw_piece = lax.all_to_all(outgoing, "sky", split_axis=0, concat_axis=0, tiled=True)
    detail_piece = lax.all_to_all(outgoing_details, "sky", split_axis=0, concat_axis=0, tiled=True)
    leading = raw_piece.shape[:2]
    flat_raw = raw_piece.reshape((-1, margin_side, margin_side))
    flat_coef = detail_piece.reshape((-1, detail_width))[:, 1 : 1 + basis_count]
    matched_piece = match_many(row_kernels, col_kernels, flat_raw, flat_coef)
    arrived = matched_piece.reshape(leading + (block_side, block_side))
    flat_match = arrived.reshape(slot_count, block_side * block_side)
    flat_info = detail_piece.reshape(slot_count, detail_width)
    cell_id = flat_info[:, basis_count + 1].astype(jnp.int32)
    band_id = flat_info[:, basis_count + 2].astype(jnp.int32)
    target_bin = band_id * CELLS + cell_id
    bin_ids = jnp.arange(BANDS * CELLS, dtype=jnp.int32)
    spread = jnp.where(
        target_bin[None, :] == bin_ids[:, None], flat_info[None, :, 0], jnp.zeros((), jnp.bfloat16)
    )
    totals = jnp.dot(spread, flat_match, preferred_element_type=jnp.float32).reshape(
        BANDS, CR, CC, block_side, block_side
    )
    weights = jnp.sum(spread.astype(jnp.float32), axis=1).reshape(BANDS, CR, CC)
    rows_here = CR // band_count
    full_totals, full_weights = lax.psum((totals, weights), "band")
    row_start = lax.axis_index("band") * rows_here
    part_totals = lax.dynamic_slice_in_dim(full_totals, row_start, rows_here, 1)
    part_weights = lax.dynamic_slice_in_dim(full_weights, row_start, rows_here, 1)
    coadd_image = part_totals / jnp.maximum(part_weights, 1.0)[..., None, None]
    combined = jnp.sum(band_gain[:, None, None, None, None] * coadd_image, axis=0)
    patch_image = (
        combined.transpose(0, 2, 1, 3)
        .reshape(rows_here * block_side, CC * block_side)
        .astype(jnp.bfloat16)
    )
    padded = extended(patch_image, (("band", 0),), radius)
    filter_bf16 = filter_taps.astype(jnp.bfloat16)
    row_filter = toeplitz(filter_bf16, rows_here * block_side)
    smoothed = jnp.dot(row_filter, padded, preferred_element_type=jnp.float32).astype(jnp.bfloat16)
    col_filter = toeplitz(filter_bf16, CC * block_side)[:, radius : radius + CC * block_side].T
    detection = jnp.dot(smoothed, col_filter, preferred_element_type=jnp.float32)
    return detection[None]


def solution(mesh):
    return jax.shard_map(
        local,
        mesh=mesh,
        in_specs=(
            P(None, ("sky", "band")),
            P(("sky", "band"), None),
            P(("sky", "band")),
            P(("sky", "band")),
            P(("sky", "band")),
            P(("sky", "band"), None),
            P(),
            P(),
            P(),
            P(),
        ),
        out_specs=P("sky", "band", None),
        check_vma=False,
    )
```

profile of v0, /device:TPU:1, one launch (start us, length us, event | category | flops | bytes accessed | tf_op | source)
XLA Modules:
  0.0 366.6 jit_solution(3276877213221580000)
XLA Ops:
  6.5 0.9 convert_reduce_fusion.1
  7.4 0.7 multiply_add_fusion.1
  8.1 0.1 fusion.39
  8.2 0.1 select_reduce_fusion
  8.3 0.7 convert_bitcast_fusion.1
  9.0 0.7 pad_maximum_fusion.2
  9.7 0.1 copy.75
  9.8 0.1 add.95
  9.9 0.6 gather_fusion
  10.5 0.7 bitcast_select_fusion
  11.2 6.4 %all-to-all-start = ((bf16[8,8,6]{2,1,0:T(8,128)(2,1)}), bf16[8,8,6]{2,1,0:T(8,128)(2,1)S(1)}, u32[]{:S(2)}, u32[]{:S(2)}) async-start(bf16[8,8,6]{2,1,0:T(8,128)(2,1)} %bitcast_select_fusion), calls=%async_computation | async-start | bytes 32768 | tf_op jit(solution)/shard_map/all_to_all | solution.py:110
  17.6 9.8 %reshape.164 = bf16[168,32,168]{2,1,0:T(8,128)(2,1)} reshape(bf16[168,5376]{1,0:T(8,128)(2,1)} %param.12) | data formatting | bytes 3612672 | tf_op jit(solution)/shard_map/reshape | solution.py:81
  27.3 3.3 copy.112
  30.6 3.4 gather_fusion.1
  34.0 5.4 %broadcast_select_fusion = bf16[8,8,168,168]{3,2,1,0:T(8,128)(2,1)} fusion(bf16[8,8,168,168]{3,2,1,0:T(8,128)(2,1)} %bitcast.119, pred[8,8]{1,0:T(8,128)(4,1)S(1)} %compare_and_fusion), kind=kLoop, calls=%fused_computation.15 | loop fusion | flops 1806336 | bytes 7225408 | tf_op jit(solution)/shard_map/jit(_take)/select_n | solution.py:106
  39.4 5.6 %all-to-all-start.1 = ((bf16[8,8,168,168]{3,2,1,0:T(8,128)(2,1)}), bf16[8,8,168,168]{3,2,1,0:T(8,128)(2,1)}, u32[]{:S(2)}, u32[]{:S(2)}) async-start(bf16[8,8,168,168]{3,2,1,0:T(8,128)(2,1)} %broadcast_select_fusion), calls=%async_computation.1 | async-start | bytes 11010048 | tf_op jit(solution)/shard_map/all_to_all | solution.py:109
  45.0 0.2 all-reduce.10.cloned.1.call-start
  45.2 0.3 tile.83
  45.6 0.2 stack_reshape.25
  45.8 0.3 tile.85
  46.1 0.2 stack_reshape.26
  46.3 0.3 tile.81
  46.7 0.2 stack_reshape.24
  46.9 0.2 copy.80
  47.1 0.3 tile.89
  47.4 0.2 stack_reshape.28
  47.7 0.3 tile.91
  48.0 0.2 stack_reshape.29
  48.2 0.3 tile.87
  48.5 0.2 stack_reshape.27
  48.8 0.2 copy.81
  49.0 0.1 slice.106
  49.0 0.1 copy.79
  49.2 0.1 fusion.46
  49.2 0.1 copy.98
  49.3 0.1 copy.99
  49.4 0.1 copy.100
  49.5 115.4 %all-to-all-done.1 = bf16[8,8,168,168]{3,2,1,0:T(8,128)(2,1)} async-done(((bf16[8,8,168,168]{3,2,1,0:T(8,128)(2,1)}), bf16[8,8,168,168]{3,2,1,0:T(8,128)(2,1)}, u32[]{:S(2)}, u32[]{:S(2)}) %all-to-all-start.1) | async-done | bytes 3612704 | tf_op jit(solution)/shard_map/all_to_all | solution.py:109
  164.9 8.3 %copy.78 = bf16[8,8,168,168]{2,3,1,0:T(8,128)(2,1)} copy(bf16[8,8,168,168]{3,2,1,0:T(8,128)(2,1)} %all-to-all-done.1) | data formatting | bytes 7225344 | tf_op jit(solution)/shard_map/all_to_all | solution.py:109
  173.2 13.1 %while.10 = (s32[]{:T(128)}, bf16[4,16,128,128]{3,2,1,0:T(8,128)(2,1)S(1)}, bf16[4,16,3]{1,2,0:T(4,128)(2,1)S(1)}, bf16[4,16,168,168]{2,3,1,0:T(8,128)(2,1)}, bf...) while((s32[]{:T(128)}, bf16[4,16,128,128]{3,2,1,0:T(8,128)(2,1)S(1)}, ...), condition=%wide.region_5.6_spmd, body=%wide.region_3.5_spmd.sunk | while | flops 613400640 | bytes 3208245 | solution.py:55
  173.2 3.1 fusion.57
  176.5 3.2 fusion.57
  179.8 3.1 fusion.57
  183.0 3.2 fusion.57
  186.3 1.4 copy.113
  187.6 0.6 copy.105
  188.2 4.9 %fusion.19 = f32[6,4,4,128,128]{4,0,3,2,1:T(8,128)} fusion(bf16[128,128,64,1,1]{1,0,2,4,3:T(8,128)(2,1)S(1)} %bitcast.120, s32[6,4,4]{0,2,1:T(4,128)S(1)} %multiply_add_fusion, s32[64]{0:T(128)S(1)} %add_bitcast_fusion, bf16[64]{0:T(256)(128)(2,1)S(1)} %bitcast.133), kind=kOutput, calls=%fused_computation.18 | convolution fusion | flops 201338880 | bytes 8389376 | tf_op jit(solution)/shard_map/dot_general | solution.py:125
  193.2 0.1 convert_reduce_fusion
  193.3 0.1 reshape.165
  193.4 0.1 copy.83
  193.5 7.5 %psum.15 = f32[6,4,4]{0,2,1:T(4,128)S(1)} all-reduce(f32[6,4,4]{0,2,1:T(4,128)S(1)} %copy.83), channel_id=1, replica_groups=mesh['sky'=8,'band'=4] {'band'}, use_global_device_ids=true, to_apply=%region_8.9 | all-reduce | flops 96 | bytes 768 | tf_op jit(solution)/shard_map/psum | solution.py:130
  201.0 145.9 %all-reduce.10.cloned.1.call-done = f32[6,4,4,128,128]{4,0,3,2,1:T(8,128)} async-done(((f32[6,4,4,128,128]{4,0,3,2,1:T(8,128)}), f32[6,4,4,128,128]{4,0,3,2,1:T(8,128)}) %all-reduce.10.cloned.1.call-update) | async-done | bytes 6291472 | tf_op jit(solution)/shard_map/psum | solution.py:130
  346.8 2.4 multiply_reduce_fusion
  349.2 0.2 copy.96
  349.5 2.8 collective-permute-start
  352.3 2.1 collective-permute-start.1
  354.5 0.9 tile.93
  355.5 1.1 reshape.166
  356.6 0.3 tile.39
  357.0 0.2 reshape.161
  357.2 0.1 copy.85
  357.3 0.1 copy.88
  357.5 1.1 collective-permute-done.1
  358.5 1.2 convolution_bitcast_fusion
  (57 shorter events, 0.8 us)
Async XLA Ops:
  11.2 28.2 %all-to-all-start = ((bf16[8,8,6]{2,1,0:T(8,128)(2,1)}), bf16[8,8,6]{2,1,0:T(8,128)(2,1)S(1)}, u32[]{:S(2)}, u32[]{:S(2)}) async-start(bf16[8,8,6]{2,1,0:T(8,128)(2,1)} %bitcast_select_fusion), calls=%async_computation | async-start | bytes 32768 | tf_op jit(solution)/shard_map/all_to_all | solution.py:110
  39.4 5.8 %copy-start = (f32[3,41]{1,0:T(4,128)S(1)}, f32[3,41]{1,0:T(4,128)}, u32[]{:S(2)}) copy-start(f32[3,41]{1,0:T(4,128)} %param.18) | copy-start | bytes 1480
  39.4 7.7 %copy-start.1 = (f32[3,41]{1,0:T(4,128)S(1)}, f32[3,41]{1,0:T(4,128)}, u32[]{:S(2)}) copy-start(f32[3,41]{1,0:T(4,128)} %param.19) | copy-start | bytes 1480
  39.4 125.5 %all-to-all-start.1 = ((bf16[8,8,168,168]{3,2,1,0:T(8,128)(2,1)}), bf16[8,8,168,168]{3,2,1,0:T(8,128)(2,1)}, u32[]{:S(2)}, u32[]{:S(2)}) async-start(bf16[8,8,168,168]{3,2,1,0:T(8,128)(2,1)} %broadcast_select_fusion), calls=%async_computation.1 | async-start | bytes 11010048 | tf_op jit(solution)/shard_map/all_to_all | solution.py:109
  45.0 301.9 %all-reduce.10.cloned.1.call-start = ((), (), s32[]{:S(2)}) async-start(), calls=%async_computation.2 | async-start | bytes 16777216 | tf_op jit(solution)/shard_map/psum | solution.py:130
  193.1 153.7 %copy-start.2 = (f32[6]{0:T(128)S(1)}, f32[6]{0:T(128)}, u32[]{:S(2)}) copy-start(f32[6]{0:T(128)} %param.20) | copy-start | bytes 76
  193.1 161.3 %copy-start.3 = (f32[41]{0:T(128)S(1)}, f32[41]{0:T(128)}, u32[]{:S(2)}) copy-start(f32[41]{0:T(128)} %param.21) | copy-start | bytes 496
  349.5 7.9 %collective-permute-start = (bf16[20,512]{1,0:T(8,128)(2,1)S(1)}, bf16[20,512]{1,0:T(8,128)(2,1)S(1)}, u32[]{:S(2)}, u32[]{:S(2)}) collective-permute-start(bf16[20,512]{1,0:T(8,128)(2,1)S(1)} %bitcast.132), channel_id=1, source_target_pairs={{0,1},{1,2},{2,3},{4,5},{5,6},{6,7},{8,9},{9,10},{10,11},{12,13},{... | collective-permute-start | bytes 61448 | tf_op jit(solution)/shard_map/ppermute | solution.py:17
  352.3 6.3 %collective-permute-start.1 = (bf16[20,512]{0,1:T(8,128)(2,1)S(1)}, bf16[20,512]{0,1:T(8,128)(2,1)S(1)}, u32[]{:S(2)}, u32[]{:S(2)}) collective-permute-start(bf16[20,512]{0,1:T(8,128)(2,1)S(1)} %bitcast.127), channel_id=1, source_target_pairs={{1,0},{2,1},{3,2},{5,4},{6,5},{7,6},{9,8},{10,9},{11,10},{13,12},{... | collective-permute-start | bytes 61448 | tf_op jit(solution)/shard_map/ppermute | solution.py:20
Sparse Core Ops, SparseCore 0:
  193.3 153.5 all-reduce.9
where the time goes:
time: 367 us
  waiting for transfers between devices  262 us (71%)
  local copies, waits for them, and re-layouts  35.2 us (10%)
  matrix products  18.8 us (5%)
  starting transfers between devices  17.1 us (5%)
  between operations  13.9 us (4%)
  other arithmetic  11.8 us (3%)
  blocking collectives  7.46 us (2%)
    psum x1, waiting for transfers between devices, local(): full_totals, full_weights = lax.psum((totals, weights), 'band')  146 us
    all_to_all x1, waiting for transfers between devices, local(): lax.all_to_all(outgoing, 'sky', split_axis=0, concat_axis=0, tiled=True)  115 us
    reshape x2, local copies, waits for them, and re-layouts, local(): raw_blocks.reshape(margin_side, block_count, margin_side).transpose(1, 0, 2)  13.1 us
    dot_general x4, matrix products, match_one(): jnp.einsum('kiq,kjq->kij', sectioned, col_kernels, preferred_element_type...  12.6 us
    all_to_all x1, local copies, waits for them, and re-layouts, local(): lax.all_to_all(outgoing, 'sky', split_axis=0, concat_axis=0, tiled=True)  8.32 us
    psum x1, blocking collectives, local(): full_totals, full_weights = lax.psum((totals, weights), 'band')  7.46 us
  transfers between devices with their start and end apart: 5, of which 3 were waited for; matrix products, arithmetic and copies ran while one was open for 8% of the time, Pallas kernels for 0%

commit v1 on v0

v1 whole, which is shorter than its diff:
```python
import functools

import jax
import jax.numpy as jnp
from jax import lax
from jax.experimental import pallas as pl
from jax.experimental.pallas import tpu as pltpu
from jax.sharding import PartitionSpec as P

BANDS = 6
CR = 4
CC = 4
CELLS = 16
VMEM = pltpu.VMEM
SMEM = pltpu.SMEM


def up(value, unit):
    return -(-value // unit) * unit


def banded(row, rows, width):
    tile = pltpu.roll(jnp.broadcast_to(row, (8, width)), 0, 1, stride=1, stride_axis=0)
    return jnp.concatenate([tile if i == 0 else pltpu.roll(tile, 8 * i, 1) for i in range(rows // 8)], axis=0)


def lanes_at(row, start, width):
    parts = [row, jnp.zeros((1, width - start - row.shape[1]), row.dtype)]
    if start:
        parts.insert(0, jnp.zeros((1, start), row.dtype))
    return jnp.concatenate(parts, axis=1)


def match_kernel(coef_ref, raw_ref, row_ref, col_ref, out_ref, rowk_ref, colk_ref):
    margin_side = raw_ref.shape[0]
    basis_count = row_ref.shape[0]
    block_count, block_side, unused = out_ref.shape
    width = colk_ref.shape[0] // basis_count
    for k in range(basis_count):
        rows = banded(lanes_at(row_ref[k : k + 1, :], 0, width), block_side, width)
        rowk_ref[k * block_side : (k + 1) * block_side, :] = rows[:, :margin_side].astype(jnp.bfloat16)
        cols = banded(lanes_at(col_ref[k : k + 1, :], 0, width), block_side, width)
        colk_ref[k * width : (k + 1) * width, :] = cols.T.astype(jnp.bfloat16)
    for n in range(block_count):
        block = raw_ref[:, n * margin_side : (n + 1) * margin_side]
        sectioned = jnp.dot(rowk_ref[...], block, preferred_element_type=jnp.float32)
        total = None
        for k in range(basis_count):
            part = (sectioned[k * block_side : (k + 1) * block_side] * coef_ref[n, k]).astype(jnp.bfloat16)
            term = jnp.dot(
                part,
                colk_ref[k * width : k * width + margin_side, :],
                preferred_element_type=jnp.float32,
            )
            total = term if total is None else total + term
        out_ref[n] = total.astype(jnp.bfloat16)


def match_blocks(raw_blocks, coef, row_basis, col_basis, block_side):
    margin_side = raw_blocks.shape[0]
    block_count = raw_blocks.shape[1] // margin_side
    basis_count = row_basis.shape[0]
    width = up(margin_side, 128)
    flops = 2 * block_count * basis_count * block_side * margin_side * (margin_side + block_side)
    return pl.pallas_call(
        match_kernel,
        out_shape=jax.ShapeDtypeStruct((block_count, block_side, block_side), jnp.bfloat16),
        in_specs=[
            pl.BlockSpec(memory_space=SMEM),
            pl.BlockSpec(memory_space=VMEM),
            pl.BlockSpec(memory_space=VMEM),
            pl.BlockSpec(memory_space=VMEM),
        ],
        out_specs=pl.BlockSpec(memory_space=VMEM),
        scratch_shapes=[
            VMEM((basis_count * block_side, margin_side), jnp.bfloat16),
            VMEM((basis_count * width, block_side), jnp.bfloat16),
        ],
        compiler_params=pltpu.CompilerParams(vmem_limit_bytes=32 << 20),
        cost_estimate=pl.CostEstimate(flops=2 * flops, bytes_accessed=4 << 20, transcendentals=0),
        name="match_blocks",
    )(coef, raw_blocks, row_basis, col_basis)


def bin_kernel(bins_ref, scale_ref, own_ref, other_ref, *rest):
    outs, acc_ref = rest[:-1], rest[-1]
    step = outs[0].shape[0]
    chunk = pl.program_id(0)
    acc_ref[...] = jnp.zeros_like(acc_ref)
    for source, blocks_ref in enumerate((own_ref, other_ref)):

        def add(n, carry, source=source, blocks_ref=blocks_ref):
            place = bins_ref[source, n] - chunk * step
            group = bins_ref[source + 2, n]

            @pl.when((place >= 0) & (place < step) & (group >= 0))
            def _():
                slot = group * step + place
                acc_ref[slot] += scale_ref[source, n] * blocks_ref[n].astype(jnp.float32)

            return carry

        lax.fori_loop(0, blocks_ref.shape[0], add, 0)
    for index, out_ref in enumerate(outs):
        out_ref[...] = acc_ref[index * step : (index + 1) * step].astype(out_ref.dtype)


def bin_blocks(bins, scale, own, other, groups, size, name):
    block_side = own.shape[1]
    step = min(size, 16)
    whole = pl.BlockSpec(own.shape, lambda g: (0, 0, 0))
    part = pl.BlockSpec((step, block_side, block_side), lambda g: (g, 0, 0))
    shape = jax.ShapeDtypeStruct((size, block_side, block_side), jnp.bfloat16)
    return pl.pallas_call(
        bin_kernel,
        grid=(size // step,),
        out_shape=[shape] * groups,
        in_specs=[pl.BlockSpec(memory_space=SMEM), pl.BlockSpec(memory_space=SMEM), whole, whole],
        out_specs=[part] * groups,
        scratch_shapes=[VMEM((groups * step, block_side, block_side), jnp.float32)],
        compiler_params=pltpu.CompilerParams(vmem_limit_bytes=40 << 20),
        cost_estimate=pl.CostEstimate(
            flops=4 * own.size, bytes_accessed=4 * own.size + 2 * groups * size * block_side**2, transcendentals=0
        ),
        name=name,
    )(bins, scale, own, other)


def filter_kernel(taps_ref, mid_ref, low_ref, high_ref, out_ref):
    cells, side, unused = mid_ref.shape
    edge = low_ref.shape[1]
    tap_count = taps_ref.shape[1]
    radius = (tap_count - 1) // 2
    taps = taps_ref[...]
    rows_in = side + 2 * edge
    row_filter = banded(lanes_at(taps, edge - radius, up(rows_in + 1, 128)), side, up(rows_in + 1, 128))
    row_filter = row_filter[:, :rows_in].astype(jnp.bfloat16)
    col_filter = banded(lanes_at(taps, side - radius, 3 * side), side, 3 * side).astype(jnp.bfloat16).T
    zero = jnp.zeros((side, side), jnp.bfloat16)
    smoothed = [zero]
    for c in range(cells):
        column = jnp.concatenate([low_ref[c], mid_ref[c], high_ref[c]], axis=0)
        smoothed.append(jnp.dot(row_filter, column, preferred_element_type=jnp.float32).astype(jnp.bfloat16))
    smoothed.append(zero)
    for c in range(cells):
        window = jnp.concatenate(smoothed[c : c + 3], axis=1)
        out_ref[:, c * side : (c + 1) * side] = jnp.dot(window, col_filter, preferred_element_type=jnp.float32)


def detect(taps, mid, low, high):
    cells, side, unused = mid.shape
    return pl.pallas_call(
        filter_kernel,
        out_shape=jax.ShapeDtypeStruct((side, cells * side), jnp.float32),
        in_specs=[pl.BlockSpec(memory_space=VMEM)] * 4,
        out_specs=pl.BlockSpec(memory_space=VMEM),
        compiler_params=pltpu.CompilerParams(vmem_limit_bytes=32 << 20),
        name="detect",
    )(taps, mid, low, high)


def swap(array, axis, bit):
    count = lax.axis_size(axis)
    return lax.ppermute(array, axis, [(i, i ^ (1 << bit)) for i in range(count)])


def halves(parts, send):
    total = None
    for part in parts:
        half = part.shape[0] // 2
        piece = part[half:] if send else part[:half]
        piece = piece.astype(jnp.float32)
        total = piece if total is None else total + piece
    return total


def local(
    raw_blocks,
    patch_of_block,
    cell_of_block,
    band_of_block,
    block_weight,
    basis_coef,
    row_basis,
    col_basis,
    band_gain,
    filter_taps,
):
    sky_count = lax.axis_size("sky")
    band_count = lax.axis_size("band")
    sky_bits = sky_count.bit_length() - 1
    band_bits = band_count.bit_length() - 1
    margin_side = raw_blocks.shape[0]
    block_count = raw_blocks.shape[1] // margin_side
    radius = (filter_taps.shape[0] - 1) // 2
    block_side = margin_side - 2 * radius
    sky_here = lax.axis_index("sky")
    band_here = lax.axis_index("band")

    key = (patch_of_block[:, 0] * BANDS + band_of_block) * CELLS + cell_of_block
    facts = jnp.stack([key.astype(jnp.float32), block_weight.astype(jnp.float32)])
    all_facts = lax.all_gather(facts, ("sky", "band"), axis=0)

    matched = match_blocks(raw_blocks, basis_coef.astype(jnp.float32), row_basis, col_basis, block_side)
    from_pair = swap(matched, "band", 0)

    here = sky_here * band_count + band_here
    pair = jnp.stack([here, here ^ 1])
    near = jnp.concatenate(
        [lax.dynamic_slice_in_dim(all_facts, here, 1, 0), lax.dynamic_slice_in_dim(all_facts, here ^ 1, 1, 0)]
    )
    near_key, near_weight = near[:, 0], near[:, 1]
    same = near_key[:, :, None, None] == all_facts[None, None, :, 0]
    weight_sum = jnp.sum(jnp.where(same, all_facts[None, None, :, 1], 0.0), axis=(2, 3))
    near_key = near_key.astype(jnp.int32)
    cell = near_key % CELLS
    band = near_key // CELLS % BANDS
    gain = jnp.sum(jnp.where(band[..., None] == jnp.arange(BANDS), band_gain, 0.0), axis=2)
    scale = gain * near_weight / jnp.maximum(weight_sum, 1.0)

    sky_off = near_key // (CELLS * BANDS) ^ sky_here
    band_off = cell // CC ^ band_here
    column = cell % CC
    half_columns = CC // 2
    sky_low = sky_off & 1
    sky_rest = jnp.zeros_like(sky_off)
    for bit in range(1, sky_bits):
        sky_rest = sky_rest * 2 + (sky_off >> bit & 1)
    band_rest = jnp.zeros_like(band_off)
    for bit in range(1, band_bits):
        band_rest = band_rest * 2 + (band_off >> bit & 1)
    rest_count = sky_count // 2
    row_count = band_count // 2
    side_a = (band_rest * 2 + sky_low) * rest_count + sky_rest
    side_b = (sky_low * row_count + band_rest) * rest_count + sky_rest
    second = column >= half_columns
    place = jnp.where(second, side_b, side_a) * half_columns + column % half_columns
    size = sky_count * row_count * half_columns // 2
    mine = band_off & 1 == 0
    sent = place >= size
    place = place % size
    group = second.astype(jnp.int32)
    sent_bins = jnp.concatenate([place, jnp.where(mine & sent, group, -1)])
    kept_bins = jnp.concatenate([place, jnp.where(mine & ~sent, group, -1)])

    send_a, send_b = bin_blocks(sent_bins, scale, matched, from_pair, 2, size, "bins_sent")
    steps_a = [("band", bit) for bit in range(1, band_bits)] + [("sky", 0)]
    steps_b = [("sky", 0)] + [("band", bit) for bit in range(1, band_bits)]
    got_a, got_b = swap(send_a, *steps_a[0]), swap(send_b, *steps_b[0])
    keep_a, keep_b = bin_blocks(kept_bins, scale, matched, from_pair, 2, size, "bins_kept")
    parts_a, parts_b = [keep_a, got_a], [keep_b, got_b]
    for step_a, step_b in zip(steps_a[1:], steps_b[1:]):
        got_a = swap(halves(parts_a, True).astype(jnp.bfloat16), *step_a)
        got_b = swap(halves(parts_b, True).astype(jnp.bfloat16), *step_b)
        parts_a = [part[: part.shape[0] // 2] for part in parts_a] + [got_a]
        parts_b = [part[: part.shape[0] // 2] for part in parts_b] + [got_b]

    def by_sky(part):
        return part.reshape((rest_count, half_columns) + part.shape[1:])

    parts_a, parts_b = [by_sky(part) for part in parts_a], [by_sky(part) for part in parts_b]
    later = []
    for bit in range(1, sky_bits):
        outgoing = jnp.concatenate([halves(parts_a, True), halves(parts_b, True)], axis=1)
        for part in later:
            outgoing = outgoing + part[part.shape[0] // 2 :].astype(jnp.float32)
        got = swap(outgoing.astype(jnp.bfloat16), "sky", bit)
        parts_a = [part[: part.shape[0] // 2] for part in parts_a]
        parts_b = [part[: part.shape[0] // 2] for part in parts_b]
        later = [part[: part.shape[0] // 2] for part in later] + [got]

    def full(parts):
        return functools.reduce(jnp.add, [part.astype(jnp.float32) for part in parts])

    combined = jnp.concatenate([full(parts_a), full(parts_b)], axis=1) + full(later)
    combined = combined[0].astype(jnp.bfloat16)

    edge = up(radius, 16)
    forward = [(i, i + 1) for i in range(band_count - 1)]
    backward = [(i + 1, i) for i in range(band_count - 1)]
    low = lax.ppermute(combined[:, block_side - edge :], "band", forward)
    high = lax.ppermute(combined[:, :edge], "band", backward)
    taps = filter_taps.astype(jnp.bfloat16).astype(jnp.float32)[None]
    return detect(taps, combined, low, high)[None]


def solution(mesh):
    return jax.shard_map(
        local,
        mesh=mesh,
        in_specs=(
            P(None, ("sky", "band")),
            P(("sky", "band"), None),
            P(("sky", "band")),
            P(("sky", "band")),
            P(("sky", "band")),
            P(("sky", "band"), None),
            P(),
            P(),
            P(),
            P(),
        ),
        out_specs=P("sky", "band", None),
        check_vma=False,
    )
```

time: 367 us -> 101 us (0.28)
  waiting for transfers between devices: 262 us -> 32.3 us
  blocking collectives: 7.46 us -> 43.1 us
  local copies, waits for them, and re-layouts: 35.2 us -> 3.68 us
  matrix products: 18.8 us -> 0 us
  between operations: 13.9 us -> 0.25 us
  other arithmetic: 11.8 us -> 1.51 us
  Pallas kernels: 0 us -> 10 us
  starting transfers between devices: 17.1 us -> 9.55 us
    psum x1 -> x0, waiting for transfers between devices: 146 us -> none  [local(): full_totals, full_weights = lax.psum((totals, weights), 'band')]
    all_to_all x2 -> x0, waiting for transfers between devices: 115 us -> none  [the longest x1 115 us: local(): lax.all_to_all(outgoing, 'sky', split_axis=0, concat_axis=0, tiled=True)]
    all_gather x0 -> x1, blocking collectives: none -> 43.1 us  [local(): all_facts = lax.all_gather(facts, ('sky', 'band'), axis=0)]
    ppermute x2 -> x9, waiting for transfers between devices: 1.09 us -> 32.3 us  [the longest x7 29 us: swap(): return lax.ppermute(array, axis, [(i, i ^ 1 << bit) for i in range(count)])]
    dot_general x6 -> x0, matrix products: 18.8 us -> none  [the longest x4 12.6 us: match_one(): jnp.einsum('kiq,kjq->kij', sectioned, col_kernels, preferred_element_type...]
    reshape x6 -> x0, local copies, waits for them, and re-layouts: 14.6 us -> none  [the longest x2 13.1 us: local(): raw_blocks.reshape(margin_side, block_count, margin_side).transpose(1, 0, 2)]
    all_to_all x2 -> x0, starting transfers between devices: 11.9 us -> none  [the longest x1 6.35 us: local(): lax.all_to_all(outgoing_details, 'sky', split_axis=0, concat_axis=0, tile...]
    pallas_call x0 -> x4, Pallas kernels: none -> 10 us  [the longest x1 4.59 us: match_blocks(): pl.pallas_call(match_kernel, out_shape=jax.ShapeDtypeStruct((block_count,...]
  transfers between devices with their start and end apart: 5 -> 9, of which waited for: 3 -> 6; matrix products, arithmetic and copies ran while one was open for 8% -> 1% of each run, Pallas kernels for 0% -> 2%
where the time goes in v1:
time: 101 us; the launch traced here: 100 us
  blocking collectives  43.1 us (43%)
  waiting for transfers between devices  32.3 us (32%)
  Pallas kernels  10 us (10%)
  starting transfers between devices  9.55 us (9%)
  local copies, waits for them, and re-layouts  3.68 us (4%)
  other arithmetic  1.51 us (1%)
    all_gather x1, blocking collectives, local(): all_facts = lax.all_gather(facts, ('sky', 'band'), axis=0)  43.1 us
    ppermute x7, waiting for transfers between devices, swap(): return lax.ppermute(array, axis, [(i, i ^ 1 << bit) for i in range(count)])  29 us
    ppermute x1, starting transfers between devices, local(): low = lax.ppermute(combined[:, block_side - edge:], 'band', forward)  6.11 us
    pallas_call x1, Pallas kernels, match_blocks(): pl.pallas_call(match_kernel, out_shape=jax.ShapeDtypeStruct((block_count,...  4.59 us
    pallas_call x2, Pallas kernels, bin_blocks(): pl.pallas_call(bin_kernel, grid=(size // step,), out_shape=[shape] * grou...  4.07 us
    ppermute x1, waiting for transfers between devices, local(): high = lax.ppermute(combined[:, :edge], 'band', backward)  3.27 us
    unnamed x18, local copies, waits for them, and re-layouts  2.88 us
  transfers between devices with their start and end apart: 9, of which 6 were waited for; matrix products, arithmetic and copies ran while one was open for 1% of the time, Pallas kernels for 2%

profile of v1, /device:TPU:1, one launch (start us, length us, event | category | flops | bytes accessed | tf_op | source)
XLA Modules:
  0.0 100.4 jit_solution(11261985068099415320)
XLA Ops:
  0.0 0.8 copy.14.coef_ref
  0.8 0.0 copy-start
  0.8 1.5 %copy-done = bf16[168,5376]{1,0:T(8,128)(2,1)S(1)} copy-done((bf16[168,5376]{1,0:T(8,128)(2,1)S(1)}, bf16[168,5376]{1,0:T(8,128)(2,1)}, u32[]{:S(2)}) %copy-start) | copy-done | bytes 1806360
  2.3 0.0 copy-start.1
  2.3 0.7 copy-done.1
  2.9 0.0 copy-start.2
  2.9 0.7 copy-done.2
  3.6 0.0 copy-start.7
  3.6 0.0 copy-start.4
  3.6 0.0 copy-start.5
  3.6 0.0 copy-start.6
  3.6 0.0 copy-start.3
  3.6 4.6 %match_blocks.1.own_ref = bf16[32,128,128]{2,1,0:T(8,128)(2,1)S(1)} custom-call(f32[32,3]{1,0:T(8,128)S(1)} %copy.14.coef_ref, bf16[168,5376]{1,0:T(8,128)(2,1)S(1)} %copy-done, f32[3,41]{1,0:T(4,128)S(1)} %copy-done.1, f32[3,41]{1,0:T(4,128)S(1)} %copy-done.2), custom_call_target="tpu_custom_call" | custom-call | flops 2444230656 | bytes 4194304 | tf_op jit(solution)/shard_map/match_blocks/pallas_call | solution.py:65
  8.2 0.1 collective-permute-start
  8.4 0.0 copy-done.7
  8.4 0.0 copy-done.4
  8.4 0.0 copy-done.5
  8.4 0.0 copy-done.6
  8.4 43.1 %all-gather.1 = f32[32,2,32]{2,1,0:T(2,128)S(1)} all-gather(f32[1,2,32]{2,1,0:T(2,128)S(1)} %maximum_bitcast_fusion), channel_id=2, replica_groups=mesh['sky'=8,'band'=4] {'sky','band'}, dimensions={0}, use_global_device_ids=true | all-gather | bytes 8448 | tf_op jit(solution)/shard_map/all_gather | solution.py:202
  51.6 0.0 copy-done.3
  51.7 0.1 fusion.3
  51.8 0.9 select_reduce_fusion
  52.6 0.0 collective-permute-done.other_ref
  52.6 2.1 %bins_sent.1 = (bf16[16,128,128]{2,1,0:T(8,128)(2,1)S(1)}, bf16[16,128,128]{2,1,0:T(8,128)(2,1)S(1)}) custom-call(s32[4,32]{1,0:T(4,128)S(1)} %get-tuple-element.30.bins_ref, f32[2,32]{1,0:T(2,128)S(1)} %maximum_divide_fusion.scale_ref, bf16[32,128,128]{2,1,0:T(8,128)(2,1)S(1)} %match_blocks.1.own_ref, bf16[32,128,128]{2,1,0:T(8,128)(2,1)S(1)} %collective-permute-done.other_ref), custom_call_target="tpu_custom_call" | custom-call | flops 2097152 | bytes 3145728 | tf_op jit(solution)/shard_map/bins_sent/pallas_call | solution.py:114
  54.7 0.1 collective-permute-start.1
  54.8 0.1 collective-permute-start.3
  54.9 2.0 %bins_kept.1 = (bf16[16,128,128]{2,1,0:T(8,128)(2,1)S(1)}, bf16[16,128,128]{2,1,0:T(8,128)(2,1)S(1)}) custom-call(s32[4,32]{1,0:T(4,128)S(1)} %get-tuple-element.29.bins_ref, f32[2,32]{1,0:T(2,128)S(1)} %maximum_divide_fusion.scale_ref, bf16[32,128,128]{2,1,0:T(8,128)(2,1)S(1)} %match_blocks.1.own_ref, bf16[32,128,128]{2,1,0:T(8,128)(2,1)S(1)} %collective-permute-done.other_ref), custom_call_target="tpu_custom_call" | custom-call | flops 2097152 | bytes 3145728 | tf_op jit(solution)/shard_map/bins_kept/pallas_call | solution.py:114
  56.9 11.3 %collective-permute-done.1 = bf16[16,128,128]{2,1,0:T(8,128)(2,1)S(1)} collective-permute-done((bf16[16,128,128]{2,1,0:T(8,128)(2,1)S(1)}, bf16[16,128,128]{2,1,0:T(8,128)(2,1)S(1)}, u32[]{:S(2)}, u32[]{:S(2)}) %collective-permute-start.1) | collective-permute-done | bytes 524320 | tf_op jit(solution)/shard_map/ppermute | solution.py:164
  68.2 0.1 add_convert_fusion.1
  68.2 0.1 collective-permute-start.2
  68.3 0.0 collective-permute-done.3
  68.3 0.1 add_convert_fusion
  68.4 1.0 %collective-permute-start.4 = (bf16[8,128,128]{2,1,0:T(8,128)(2,1)S(1)}, bf16[8,128,128]{2,1,0:T(8,128)(2,1)S(1)}, u32[]{:S(2)}, u32[]{:S(2)}) collective-permute-start(bf16[8,128,128]{2,1,0:T(8,128)(2,1)S(1)} %add_convert_fusion), channel_id=1, source_target_pairs={{0,2},{1,3},{2,0},{3,1},{4,6},{5,7},{6,4},{7,5},{8,10},{9,11},{10,... | collective-permute-start | bytes 786440 | tf_op jit(solution)/shard_map/ppermute | solution.py:164
  69.5 5.7 %collective-permute-done.2 = bf16[8,128,128]{2,1,0:T(8,128)(2,1)S(1)} collective-permute-done((bf16[8,128,128]{2,1,0:T(8,128)(2,1)S(1)}, bf16[8,128,128]{2,1,0:T(8,128)(2,1)S(1)}, u32[]{:S(2)}, u32[]{:S(2)}) %collective-permute-start.2) | collective-permute-done | bytes 262176 | tf_op jit(solution)/shard_map/ppermute | solution.py:164
  75.2 0.1 add_convert_fusion.3
  75.2 0.0 copy-start.8
  75.2 0.1 collective-permute-done.4
  75.3 0.1 add_convert_fusion.2
  75.4 0.1 collective-permute-start.5
  75.5 0.1 add_bitcast_fusion.3
  75.6 0.1 add_bitcast_fusion.2
  75.6 5.8 %collective-permute-done.5 = bf16[2,4,128,128]{3,2,1,0:T(8,128)(2,1)S(1)} collective-permute-done((bf16[2,4,128,128]{3,2,1,0:T(8,128)(2,1)S(1)}, bf16[2,4,128,128]{3,2,1,0:T(8,128)(2,1)S(1)}, u32[]{:S(2)}, u32[]{:S(2)}) %collective-permute-start.5) | collective-permute-done | bytes 262176 | tf_op jit(solution)/shard_map/ppermute | solution.py:164
  81.4 0.1 collective-permute-start.6
  81.5 6.1 %collective-permute-done.6 = bf16[1,4,128,128]{3,2,1,0:T(8,128)(2,1)S(1)} collective-permute-done((bf16[1,4,128,128]{3,2,1,0:T(8,128)(2,1)S(1)}, bf16[1,4,128,128]{3,2,1,0:T(8,128)(2,1)S(1)}, u32[]{:S(2)}, u32[]{:S(2)}) %collective-permute-start.6) | collective-permute-done | bytes 131104 | tf_op jit(solution)/shard_map/ppermute | solution.py:164
  87.6 0.1 fusion.2.mid_ref
  87.7 6.1 %collective-permute-start.7 = (bf16[4,32,128]{2,1,0:T(8,128)(2,1)S(1)}, bf16[4,32,128]{2,1,0:T(8,128)(2,1)S(1)}, u32[]{:S(2)}, u32[]{:S(2)}) collective-permute-start(bf16[4,32,128]{2,1,0:T(8,128)(2,1)S(1)} %get-tuple-element.22), channel_id=1, source_target_pairs={{0,1},{1,2},{2,3},{4,5},{5,6},{6,7},{8,9},{9,10},{10,11},{12,13},{... | collective-permute-start | bytes 98312 | tf_op jit(solution)/shard_map/ppermute | solution.py:281
  93.8 1.9 %collective-permute-start.8 = (bf16[4,32,128]{2,1,0:T(8,128)(2,1)S(1)}, bf16[4,32,128]{2,1,0:T(8,128)(2,1)S(1)}, u32[]{:S(2)}, u32[]{:S(2)}) collective-permute-start(bf16[4,32,128]{2,1,0:T(8,128)(2,1)S(1)} %get-tuple-element.21), channel_id=1, source_target_pairs={{1,0},{2,1},{3,2},{5,4},{6,5},{7,6},{9,8},{10,9},{11,10},{13,12},{... | collective-permute-start | bytes 98312 | tf_op jit(solution)/shard_map/ppermute | solution.py:282
  95.8 0.0 copy-done.8
  95.8 0.0 collective-permute-done.7.low_ref
  95.8 3.3 %collective-permute-done.8.high_ref = bf16[4,32,128]{2,1,0:T(8,128)(2,1)S(1)} collective-permute-done((bf16[4,32,128]{2,1,0:T(8,128)(2,1)S(1)}, bf16[4,32,128]{2,1,0:T(8,128)(2,1)S(1)}, u32[]{:S(2)}, u32[]{:S(2)}) %collective-permute-start.8) | collective-permute-done | bytes 32800 | tf_op jit(solution)/shard_map/ppermute | solution.py:282
  99.1 1.4 %detect.1 = f32[128,512]{1,0:T(8,128)} custom-call(f32[1,41]{1,0:T(1,128)S(1)} %bitcast_convert_fusion.1.taps_ref, bf16[4,128,128]{2,1,0:T(8,128)(2,1)S(1)} %fusion.2.mid_ref, bf16[4,32,128]{2,1,0:T(8,128)(2,1)S(1)} %collective-permute-done.7.low_ref, bf16[4,32,128]{2,1,0:T(8,128)(2,1)S(1)} %collective-permute-done.8.high_ref), custom_call_target="tpu_custom_call" | custom-call | tf_op jit(solution)/shard_map/detect/pallas_call | solution.py:152
  (14 shorter events, 0.2 us)
Async XLA Ops:
  0.8 1.5 %copy-start = (bf16[168,5376]{1,0:T(8,128)(2,1)S(1)}, bf16[168,5376]{1,0:T(8,128)(2,1)}, u32[]{:S(2)}) copy-start(bf16[168,5376]{1,0:T(8,128)(2,1)} %raw_ref.1) | copy-start | bytes 5419012
  2.3 0.7 copy-start.1
  2.9 0.7 copy-start.2
  3.6 4.7 %copy-start.7 = (bf16[32]{0:T(256)(128)(2,1)S(1)}, bf16[32]{0:T(256)(128)(2,1)}, u32[]{:S(2)}) copy-start(bf16[32]{0:T(256)(128)(2,1)} %param.14) | copy-start | bytes 196
  3.6 4.8 %copy-start.4 = (s32[32]{0:T(128)S(1)}, s32[32]{0:T(128)}, u32[]{:S(2)}) copy-start(s32[32]{0:T(128)} %param.12) | copy-start | bytes 388
  3.6 4.8 %copy-start.5 = (s32[32]{0:T(128)S(1)}, s32[32]{0:T(128)}, u32[]{:S(2)}) copy-start(s32[32]{0:T(128)} %param.13) | copy-start | bytes 388
  3.6 4.8 %copy-start.6 = (s32[32,1]{0,1:T(1,128)S(1)}, s32[32,1]{0,1:T(1,128)}, u32[]{:S(2)}) copy-start(s32[32,1]{0,1:T(1,128)} %param.11) | copy-start | bytes 388
  3.6 48.0 %copy-start.3 = (f32[6]{0:T(128)S(1)}, f32[6]{0:T(128)}, u32[]{:S(2)}) copy-start(f32[6]{0:T(128)} %param.18) | copy-start | bytes 76
  8.2 44.4 %collective-permute-start = (bf16[32,128,128]{2,1,0:T(8,128)(2,1)S(1)}, bf16[32,128,128]{2,1,0:T(8,128)(2,1)S(1)}, u32[]{:S(2)}, u32[]{:S(2)}) collective-permute-start(bf16[32,128,128]{2,1,0:T(8,128)(2,1)S(1)} %match_blocks.1.own_ref), channel_id=1, source_target_pairs={{0,1},{1,0},{2,3},{3,2},{4,5},{5,4},{6,7},{7,6},{8,9},{9,8},{10,11... | collective-permute-start | bytes 3145736 | tf_op jit(solution)/shard_map/ppermute | solution.py:164
  54.7 13.4 %collective-permute-start.1 = (bf16[16,128,128]{2,1,0:T(8,128)(2,1)S(1)}, bf16[16,128,128]{2,1,0:T(8,128)(2,1)S(1)}, u32[]{:S(2)}, u32[]{:S(2)}) collective-permute-start(bf16[16,128,128]{2,1,0:T(8,128)(2,1)S(1)} %get-tuple-element.10), channel_id=1, source_target_pairs={{0,2},{1,3},{2,0},{3,1},{4,6},{5,7},{6,4},{7,5},{8,10},{9,11},{10,... | collective-permute-start | bytes 1572872 | tf_op jit(solution)/shard_map/ppermute | solution.py:164
  54.8 13.5 %collective-permute-start.3 = (bf16[16,128,128]{2,1,0:T(8,128)(2,1)S(1)}, bf16[16,128,128]{2,1,0:T(8,128)(2,1)S(1)}, u32[]{:S(2)}, u32[]{:S(2)}) collective-permute-start(bf16[16,128,128]{2,1,0:T(8,128)(2,1)S(1)} %get-tuple-element.12), channel_id=1, source_target_pairs={{0,4},{4,0},{8,12},{12,8},{16,20},{20,16},{24,28},{28,24},{1,5},{5... | collective-permute-start | bytes 1572872 | tf_op jit(solution)/shard_map/ppermute | solution.py:164
  68.2 6.9 %collective-permute-start.2 = (bf16[8,128,128]{2,1,0:T(8,128)(2,1)S(1)}, bf16[8,128,128]{2,1,0:T(8,128)(2,1)S(1)}, u32[]{:S(2)}, u32[]{:S(2)}) collective-permute-start(bf16[8,128,128]{2,1,0:T(8,128)(2,1)S(1)} %add_convert_fusion.1), channel_id=1, source_target_pairs={{0,4},{4,0},{8,12},{12,8},{16,20},{20,16},{24,28},{28,24},{1,5},{5... | collective-permute-start | bytes 786440 | tf_op jit(solution)/shard_map/ppermute | solution.py:164
  68.4 6.9 %collective-permute-start.4 = (bf16[8,128,128]{2,1,0:T(8,128)(2,1)S(1)}, bf16[8,128,128]{2,1,0:T(8,128)(2,1)S(1)}, u32[]{:S(2)}, u32[]{:S(2)}) collective-permute-start(bf16[8,128,128]{2,1,0:T(8,128)(2,1)S(1)} %add_convert_fusion), channel_id=1, source_target_pairs={{0,2},{1,3},{2,0},{3,1},{4,6},{5,7},{6,4},{7,5},{8,10},{9,11},{10,... | collective-permute-start | bytes 786440 | tf_op jit(solution)/shard_map/ppermute | solution.py:164
  75.2 20.5 %copy-start.8 = (f32[41]{0:T(128)S(1)}, f32[41]{0:T(128)}, u32[]{:S(2)}) copy-start(f32[41]{0:T(128)} %param.19) | copy-start | bytes 496
  75.4 6.0 %collective-permute-start.5 = (bf16[2,4,128,128]{3,2,1,0:T(8,128)(2,1)S(1)}, bf16[2,4,128,128]{3,2,1,0:T(8,128)(2,1)S(1)}, u32[]{:S(2)}, u32[]{:S(2)}) collective-permute-start(bf16[2,4,128,128]{3,2,1,0:T(8,128)(2,1)S(1)} %pad_maximum_fusion), channel_id=1, source_target_pairs={{0,8},{4,12},{8,0},{12,4},{16,24},{20,28},{24,16},{28,20},{1,9},{5... | collective-permute-start | bytes 786440 | tf_op jit(solution)/shard_map/ppermute | solution.py:164
  81.4 6.2 %collective-permute-start.6 = (bf16[1,4,128,128]{3,2,1,0:T(8,128)(2,1)S(1)}, bf16[1,4,128,128]{3,2,1,0:T(8,128)(2,1)S(1)}, u32[]{:S(2)}, u32[]{:S(2)}) collective-permute-start(bf16[1,4,128,128]{3,2,1,0:T(8,128)(2,1)S(1)} %fusion.1), channel_id=1, source_target_pairs={{0,16},{4,20},{8,24},{12,28},{16,0},{20,4},{24,8},{28,12},{1,17},{... | collective-permute-start | bytes 393224 | tf_op jit(solution)/shard_map/ppermute | solution.py:164
  87.7 8.1 %collective-permute-start.7 = (bf16[4,32,128]{2,1,0:T(8,128)(2,1)S(1)}, bf16[4,32,128]{2,1,0:T(8,128)(2,1)S(1)}, u32[]{:S(2)}, u32[]{:S(2)}) collective-permute-start(bf16[4,32,128]{2,1,0:T(8,128)(2,1)S(1)} %get-tuple-element.22), channel_id=1, source_target_pairs={{0,1},{1,2},{2,3},{4,5},{5,6},{6,7},{8,9},{9,10},{10,11},{12,13},{... | collective-permute-start | bytes 98312 | tf_op jit(solution)/shard_map/ppermute | solution.py:281
  93.8 5.2 %collective-permute-start.8 = (bf16[4,32,128]{2,1,0:T(8,128)(2,1)S(1)}, bf16[4,32,128]{2,1,0:T(8,128)(2,1)S(1)}, u32[]{:S(2)}, u32[]{:S(2)}) collective-permute-start(bf16[4,32,128]{2,1,0:T(8,128)(2,1)S(1)} %get-tuple-element.21), channel_id=1, source_target_pairs={{1,0},{2,1},{3,2},{5,4},{6,5},{7,6},{9,8},{10,9},{11,10},{13,12},{... | collective-permute-start | bytes 98312 | tf_op jit(solution)/shard_map/ppermute | solution.py:282

commit v2 on v1

--- a/solution.py
+++ b/solution.py
@@ -31,29 +31,42 @@
     return jnp.concatenate(parts, axis=1)
 
 
-def match_kernel(coef_ref, raw_ref, row_ref, col_ref, out_ref, rowk_ref, colk_ref):
+def match_part(raw_ref, coef_ref, rowk_ref, colk_ref, out_ref):
     margin_side = raw_ref.shape[0]
+    basis_count = coef_ref.shape[1]
+    block_count, block_side, unused = out_ref.shape
+    width = colk_ref.shape[0] // basis_count
+    coef = coef_ref[...].astype(jnp.float32)
+    for n in range(block_count):
+        block = raw_ref[:, n * margin_side : (n + 1) * margin_side]
+        sectioned = jnp.dot(rowk_ref[...], block, preferred_element_type=jnp.float32)
+        total = None
+        for k in range(basis_count):
+            part = sectioned[k * block_side : (k + 1) * block_side] * coef[n : n + 1, k : k + 1]
+            term = jnp.dot(
+                part.astype(jnp.bfloat16),
+                colk_ref[k * width : k * width + margin_side, :],
+                preferred_element_type=jnp.float32,
+            )
+            total = term if total is None else total + term
+        out_ref[n] = total.astype(jnp.bfloat16)
+
+
+def match_first(coef_ref, raw_ref, row_ref, col_ref, out_ref, rowk_ref, colk_ref):
     basis_count = row_ref.shape[0]
-    block_count, block_side, unused = out_ref.shape
+    margin_side = raw_ref.shape[0]
+    block_side = out_ref.shape[1]
     width = colk_ref.shape[0] // basis_count
     for k in range(basis_count):
         rows = banded(lanes_at(row_ref[k : k + 1, :], 0, width), block_side, width)
         rowk_ref[k * block_side : (k + 1) * block_side, :] = rows[:, :margin_side].astype(jnp.bfloat16)
         cols = banded(lanes_at(col_ref[k : k + 1, :], 0, width), block_side, width)
         colk_ref[k * width : (k + 1) * width, :] = cols.T.astype(jnp.bfloat16)
-    for n in range(block_count):
-        block = raw_ref[:, n * margin_side : (n + 1) * margin_side]
-        sectioned = jnp.dot(rowk_ref[...], block, preferred_element_type=jnp.float32)
-        total = None
-        for k in range(basis_count):
-            part = (sectioned[k * block_side : (k + 1) * block_side] * coef_ref[n, k]).astype(jnp.bfloat16)
-            term = jnp.dot(
-                part,
-                colk_ref[k * width : k * width + margin_side, :],
-                preferred_element_type=jnp.float32,
-            )
-            total = term if total is None else total + term
-        out_ref[n] = total.astype(jnp.bfloat16)
+    match_part(raw_ref, coef_ref, rowk_ref, colk_ref, out_ref)
+
+
+def match_next(coef_ref, raw_ref, rowk_ref, colk_ref, out_ref):
+    match_part(raw_ref, coef_ref, rowk_ref, colk_ref, out_ref)
 
 
 def match_blocks(raw_blocks, coef, row_basis, col_basis, block_side):
@@ -61,37 +74,54 @@
     block_count = raw_blocks.shape[1] // margin_side
     basis_count = row_basis.shape[0]
     width = up(margin_side, 128)
-    flops = 2 * block_count * basis_count * block_side * margin_side * (margin_side + block_side)
-    return pl.pallas_call(
-        match_kernel,
-        out_shape=jax.ShapeDtypeStruct((block_count, block_side, block_side), jnp.bfloat16),
-        in_specs=[
-            pl.BlockSpec(memory_space=SMEM),
-            pl.BlockSpec(memory_space=VMEM),
-            pl.BlockSpec(memory_space=VMEM),
-            pl.BlockSpec(memory_space=VMEM),
-        ],
-        out_specs=pl.BlockSpec(memory_space=VMEM),
-        scratch_shapes=[
-            VMEM((basis_count * block_side, margin_side), jnp.bfloat16),
-            VMEM((basis_count * width, block_side), jnp.bfloat16),
-        ],
-        compiler_params=pltpu.CompilerParams(vmem_limit_bytes=32 << 20),
-        cost_estimate=pl.CostEstimate(flops=2 * flops, bytes_accessed=4 << 20, transcendentals=0),
-        name="match_blocks",
-    )(coef, raw_blocks, row_basis, col_basis)
-
-
-def bin_kernel(bins_ref, scale_ref, own_ref, other_ref, *rest):
-    outs, acc_ref = rest[:-1], rest[-1]
+    count = 16 if block_count % 16 == 0 else block_count
+    flops = 2 * count * basis_count * block_side * margin_side * (margin_side + block_side)
+
+    def fixed(*place):
+        return lambda g: place
+
+    whole = [
+        pl.BlockSpec((basis_count * block_side, margin_side), fixed(0, 0)),
+        pl.BlockSpec((basis_count * width, block_side), fixed(0, 0)),
+    ]
+    out_spec = pl.BlockSpec((count, block_side, block_side), fixed(0, 0, 0))
+    out_shape = jax.ShapeDtypeStruct((count, block_side, block_side), jnp.bfloat16)
+    results, kernels = [], ()
+    for part in range(block_count // count):
+        first = part == 0
+        basis = pl.BlockSpec(row_basis.shape, fixed(0, 0))
+        found = pl.pallas_call(
+            match_first if first else match_next,
+            grid=(1,),
+            out_shape=[
+                out_shape,
+                jax.ShapeDtypeStruct((basis_count * block_side, margin_side), jnp.bfloat16),
+                jax.ShapeDtypeStruct((basis_count * width, block_side), jnp.bfloat16),
+            ] if first else [out_shape],
+            in_specs=[
+                pl.BlockSpec((count, basis_count), fixed(part, 0)),
+                pl.BlockSpec((margin_side, count * margin_side), fixed(0, part)),
+            ] + ([basis, basis] if first else whole),
+            out_specs=[out_spec] + (whole if first else []),
+            compiler_params=pltpu.CompilerParams(vmem_limit_bytes=40 << 20),
+            cost_estimate=pl.CostEstimate(flops=2 * flops, bytes_accessed=2 << 20, transcendentals=0),
+            name="match_blocks",
+        )(coef, raw_blocks, *((row_basis, col_basis) if first else kernels))
+        results.append(found[0])
+        kernels = kernels or tuple(found[1:])
+    return results
+
+
+def bin_kernel(sources, bins_ref, scale_ref, *rest):
+    blocks_refs, outs, acc_ref = rest[:sources], rest[sources:-1], rest[-1]
     step = outs[0].shape[0]
     chunk = pl.program_id(0)
     acc_ref[...] = jnp.zeros_like(acc_ref)
-    for source, blocks_ref in enumerate((own_ref, other_ref)):
+    for source, blocks_ref in enumerate(blocks_refs):
 
         def add(n, carry, source=source, blocks_ref=blocks_ref):
             place = bins_ref[source, n] - chunk * step
-            group = bins_ref[source + 2, n]
+            group = bins_ref[source + sources, n]
 
             @pl.when((place >= 0) & (place < step) & (group >= 0))
             def _():
@@ -105,25 +135,24 @@
         out_ref[...] = acc_ref[index * step : (index + 1) * step].astype(out_ref.dtype)
 
 
-def bin_blocks(bins, scale, own, other, groups, size, name):
-    block_side = own.shape[1]
+def bin_blocks(bins, scale, blocks, groups, size, name):
+    count, block_side, unused = blocks[0].shape
     step = min(size, 16)
-    whole = pl.BlockSpec(own.shape, lambda g: (0, 0, 0))
+    whole = pl.BlockSpec(blocks[0].shape, lambda g: (0, 0, 0))
     part = pl.BlockSpec((step, block_side, block_side), lambda g: (g, 0, 0))
     shape = jax.ShapeDtypeStruct((size, block_side, block_side), jnp.bfloat16)
+    moved = 2 * len(blocks) * blocks[0].size + 2 * groups * size * block_side**2
     return pl.pallas_call(
-        bin_kernel,
+        functools.partial(bin_kernel, len(blocks)),
         grid=(size // step,),
         out_shape=[shape] * groups,
-        in_specs=[pl.BlockSpec(memory_space=SMEM), pl.BlockSpec(memory_space=SMEM), whole, whole],
+        in_specs=[pl.BlockSpec(memory_space=SMEM), pl.BlockSpec(memory_space=SMEM)] + [whole] * len(blocks),
         out_specs=[part] * groups,
         scratch_shapes=[VMEM((groups * step, block_side, block_side), jnp.float32)],
         compiler_params=pltpu.CompilerParams(vmem_limit_bytes=40 << 20),
-        cost_estimate=pl.CostEstimate(
-            flops=4 * own.size, bytes_accessed=4 * own.size + 2 * groups * size * block_side**2, transcendentals=0
-        ),
+        cost_estimate=pl.CostEstimate(flops=2 * moved, bytes_accessed=moved, transcendentals=0),
         name=name,
-    )(bins, scale, own, other)
+    )(bins, scale, *blocks)
 
 
 def filter_kernel(taps_ref, mid_ref, low_ref, high_ref, out_ref):
@@ -198,20 +227,17 @@
     band_here = lax.axis_index("band")
 
     key = (patch_of_block[:, 0] * BANDS + band_of_block) * CELLS + cell_of_block
-    facts = jnp.stack([key.astype(jnp.float32), block_weight.astype(jnp.float32)])
-    all_facts = lax.all_gather(facts, ("sky", "band"), axis=0)
-
-    matched = match_blocks(raw_blocks, basis_coef.astype(jnp.float32), row_basis, col_basis, block_side)
-    from_pair = swap(matched, "band", 0)
-
-    here = sky_here * band_count + band_here
-    pair = jnp.stack([here, here ^ 1])
-    near = jnp.concatenate(
-        [lax.dynamic_slice_in_dim(all_facts, here, 1, 0), lax.dynamic_slice_in_dim(all_facts, here ^ 1, 1, 0)]
-    )
-    near_key, near_weight = near[:, 0], near[:, 1]
-    same = near_key[:, :, None, None] == all_facts[None, None, :, 0]
-    weight_sum = jnp.sum(jnp.where(same, all_facts[None, None, :, 1], 0.0), axis=(2, 3))
+    facts = jnp.stack([key.astype(jnp.float32), block_weight.astype(jnp.float32)])[None]
+    for axis, bits in (("band", band_bits), ("sky", sky_bits)):
+        for bit in range(bits):
+            facts = jnp.concatenate([facts, swap(facts, axis, bit)])
+
+    matched = match_blocks(raw_blocks, basis_coef, row_basis, col_basis, block_side)
+    from_pair = [swap(part, "band", 0) for part in matched]
+
+    near_key, near_weight = facts[:2, 0], facts[:2, 1]
+    same = near_key[:, :, None, None] == facts[None, None, :, 0]
+    weight_sum = jnp.sum(jnp.where(same, facts[None, None, :, 1], 0.0), axis=(2, 3))
     near_key = near_key.astype(jnp.int32)
     cell = near_key % CELLS
     band = near_key // CELLS % BANDS
@@ -240,14 +266,19 @@
     sent = place >= size
     place = place % size
     group = second.astype(jnp.int32)
-    sent_bins = jnp.concatenate([place, jnp.where(mine & sent, group, -1)])
-    kept_bins = jnp.concatenate([place, jnp.where(mine & ~sent, group, -1)])
-
-    send_a, send_b = bin_blocks(sent_bins, scale, matched, from_pair, 2, size, "bins_sent")
+    near_blocks = matched + from_pair
+    scale, place, sent_group, kept_group = (
+        value.reshape(len(near_blocks), -1)
+        for value in (scale, place, jnp.where(mine & sent, group, -1), jnp.where(mine & ~sent, group, -1))
+    )
+    sent_bins = jnp.concatenate([place, sent_group])
+    kept_bins = jnp.concatenate([place, kept_group])
+
+    send_a, send_b = bin_blocks(sent_bins, scale, near_blocks, 2, size, "bins_sent")
     steps_a = [("band", bit) for bit in range(1, band_bits)] + [("sky", 0)]
     steps_b = [("sky", 0)] + [("band", bit) for bit in range(1, band_bits)]
     got_a, got_b = swap(send_a, *steps_a[0]), swap(send_b, *steps_b[0])
-    keep_a, keep_b = bin_blocks(kept_bins, scale, matched, from_pair, 2, size, "bins_kept")
+    keep_a, keep_b = bin_blocks(kept_bins, scale, near_blocks, 2, size, "bins_kept")
     parts_a, parts_b = [keep_a, got_a], [keep_b, got_b]
     for step_a, step_b in zip(steps_a[1:], steps_b[1:]):
         got_a = swap(halves(parts_a, True).astype(jnp.bfloat16), *step_a)

time: 101 us -> 73.7 us (0.73)
  blocking collectives: 43.1 us -> 0 us
  starting transfers between devices: 9.55 us -> 29.6 us
  waiting for transfers between devices: 32.3 us -> 25.9 us
  other arithmetic: 1.51 us -> 2.92 us
    all_gather x1 -> x0, blocking collectives: 43.1 us -> none  [local(): all_facts = lax.all_gather(facts, ('sky', 'band'), axis=0)]
    ppermute x7 -> x13, starting transfers between devices: 1.52 us -> 17.2 us  [swap(): return lax.ppermute(array, axis, [(i, i ^ 1 << bit) for i in range(count)])]
    ppermute x7 -> x13, waiting for transfers between devices: 29 us -> 22.7 us  [swap(): return lax.ppermute(array, axis, [(i, i ^ 1 << bit) for i in range(count)])]
    ppermute x1, starting transfers between devices: 6.11 us -> 10.4 us  [local(): low = lax.ppermute(combined[:, block_side - edge:], 'band', forward)]
    another operation x4, other arithmetic: 0.12 us -> 1.46 us  [the longest x2 1.35 us: local(): jnp.stack([key.astype(jnp.float32), block_weight.astype(jnp.float32)])[None]]
    unnamed x18 -> x14, local copies, waits for them, and re-layouts: 2.88 us -> 3.66 us
    pallas_call x3 -> x4, Pallas kernels: 8.66 us -> 8.76 us  [the longest x2 4.55 us: match_blocks(): pl.pallas_call(match_first if first else match_next, grid=(1,), out_shape...]
  transfers between devices with their start and end apart: 9 -> 15, of which waited for: 6 -> 9; matrix products, arithmetic and copies ran while one was open for 1% -> 4% of each run, Pallas kernels for 2% -> 9%
where the time goes in v2:
time: 73.7 us; the launch traced here: 72.8 us
  starting transfers between devices  29.6 us (40%)
  waiting for transfers between devices  25.9 us (35%)
  Pallas kernels  10.1 us (14%)
  local copies, waits for them, and re-layouts  4.05 us (5%)
  other arithmetic  2.92 us (4%)
    ppermute x13, waiting for transfers between devices, swap(): return lax.ppermute(array, axis, [(i, i ^ 1 << bit) for i in range(count)])  22.7 us
    ppermute x13, starting transfers between devices, swap(): return lax.ppermute(array, axis, [(i, i ^ 1 << bit) for i in range(count)])  17.2 us
    ppermute x1, starting transfers between devices, local(): low = lax.ppermute(combined[:, block_side - edge:], 'band', forward)  10.4 us
    pallas_call x2, Pallas kernels, match_blocks(): pl.pallas_call(match_first if first else match_next, grid=(1,), out_shape...  4.55 us
    pallas_call x2, Pallas kernels, bin_blocks(): pl.pallas_call(functools.partial(bin_kernel, len(blocks)), grid=(size //...  4.21 us
    unnamed x14, local copies, waits for them, and re-layouts  3.66 us
    ppermute x1, waiting for transfers between devices, local(): high = lax.ppermute(combined[:, :edge], 'band', backward)  3.27 us
    ppermute x1, starting transfers between devices, local(): high = lax.ppermute(combined[:, :edge], 'band', backward)  1.92 us
  transfers between devices with their start and end apart: 15, of which 9 were waited for; matrix products, arithmetic and copies ran while one was open for 4% of the time, Pallas kernels for 9%

profile of v2, /device:TPU:1, one launch (start us, length us, event | category | flops | bytes accessed | tf_op | source)
XLA Modules:
  0.0 72.8 jit_solution(11067441303910522820)
XLA Ops:
  0.0 0.7 bitcast_convert_fusion
  0.7 0.7 convert_bitcast_fusion
  1.4 0.1 collective-permute-start
  1.5 0.8 %copy.13.coef_ref = bf16[32,3]{1,0:T(8,128)(2,1)S(1)} copy(bf16[32,3]{0,1:T(4,128)(2,1)} %param.15) | data formatting | bytes 384 | tf_op args[5]
  2.3 0.0 copy-start
  2.3 1.5 %copy-done = bf16[168,5376]{1,0:T(8,128)(2,1)S(1)} copy-done((bf16[168,5376]{1,0:T(8,128)(2,1)S(1)}, bf16[168,5376]{1,0:T(8,128)(2,1)}, u32[]{:S(2)}) %copy-start) | copy-done | bytes 1806360
  3.7 0.0 copy-start.1
  3.8 0.7 copy-done.1
  4.4 0.0 copy-start.2
  4.4 0.7 copy-done.2
  5.1 2.4 %match_blocks.2 = (bf16[16,128,128]{2,1,0:T(8,128)(2,1)S(1)}, bf16[384,168]{1,0:T(8,128)(2,1)S(1)}, bf16[768,128]{1,0:T(8,128)(2,1)S(1)}) custom-call(bf16[32,3]{1,0:T(8,128)(2,1)S(1)} %copy.13.coef_ref, bf16[168,5376]{1,0:T(8,128)(2,1)S(1)} %copy-done, f32[3,41]{1,0:T(4,128)S(1)} %copy-done.1, f32[3,41]{1,0:T(4,128)S(1)} %copy-done.2), custom_call_target="tpu_custom_call" | custom-call | flops 1222115328 | bytes 2097152 | tf_op jit(solution)/shard_map/match_blocks/pallas_call | solution.py:93
  7.5 0.0 copy-start.3
  7.5 2.2 %match_blocks.3.rest_1_ = bf16[16,128,128]{2,1,0:T(8,128)(2,1)S(1)} custom-call(bf16[32,3]{1,0:T(8,128)(2,1)S(1)} %copy.13.coef_ref, bf16[168,5376]{1,0:T(8,128)(2,1)S(1)} %copy-done, bf16[384,168]{1,0:T(8,128)(2,1)S(1)} %get-tuple-element.13.rowk_ref, bf16[768,128]{1,0:T(8,128)(2,1)S(1)} %get-tuple-element.14.colk_ref), custom_call_target="tpu_custom_call" | custom-call | flops 1222115328 | bytes 2097152 | tf_op jit(solution)/shard_map/match_blocks/pallas_call | solution.py:93
  9.7 0.5 collective-permute-start.6
  10.2 0.1 collective-permute-start.5
  10.3 0.0 collective-permute-done
  10.3 2.7 %collective-permute-start.1 = (f32[2,2,32]{2,1,0:T(2,128)S(1)}, f32[2,2,32]{2,1,0:T(2,128)S(1)}, u32[]{:S(2)}, u32[]{:S(2)}) collective-permute-start(f32[2,2,32]{2,1,0:T(2,128)S(1)} %pad_maximum_fusion.3), channel_id=1, source_target_pairs={{0,2},{1,3},{2,0},{3,1},{4,6},{5,7},{6,4},{7,5},{8,10},{9,11},{10,... | collective-permute-start | bytes 1544 | tf_op jit(solution)/shard_map/ppermute | solution.py:193
  13.1 0.1 convert_element_type.139
  13.2 0.0 copy-done.3
  13.2 0.1 fusion.3
  13.3 0.7 collective-permute-done.1
  14.0 1.5 %collective-permute-start.2 = (f32[4,2,32]{2,1,0:T(2,128)S(1)}, f32[4,2,32]{2,1,0:T(2,128)S(1)}, u32[]{:S(2)}, u32[]{:S(2)}) collective-permute-start(f32[4,2,32]{2,1,0:T(2,128)S(1)} %pad_maximum_fusion.2), channel_id=1, source_target_pairs={{0,4},{4,0},{8,12},{12,8},{16,20},{20,16},{24,28},{28,24},{1,5},{5... | collective-permute-start | bytes 3080 | tf_op jit(solution)/shard_map/ppermute | solution.py:193
  15.5 1.0 %collective-permute-done.2 = f32[4,2,32]{2,1,0:T(2,128)S(1)} collective-permute-done((f32[4,2,32]{2,1,0:T(2,128)S(1)}, f32[4,2,32]{2,1,0:T(2,128)S(1)}, u32[]{:S(2)}, u32[]{:S(2)}) %collective-permute-start.2) | collective-permute-done | bytes 1056 | tf_op jit(solution)/shard_map/ppermute | solution.py:193
  16.5 1.6 %collective-permute-start.3 = (f32[8,2,32]{2,1,0:T(2,128)S(1)}, f32[8,2,32]{2,1,0:T(2,128)S(1)}, u32[]{:S(2)}, u32[]{:S(2)}) collective-permute-start(f32[8,2,32]{2,1,0:T(2,128)S(1)} %pad_maximum_fusion.1), channel_id=1, source_target_pairs={{0,8},{4,12},{8,0},{12,4},{16,24},{20,28},{24,16},{28,20},{1,9},{5... | collective-permute-start | bytes 6152 | tf_op jit(solution)/shard_map/ppermute | solution.py:193
  18.1 1.0 %collective-permute-done.3 = f32[8,2,32]{2,1,0:T(2,128)S(1)} collective-permute-done((f32[8,2,32]{2,1,0:T(2,128)S(1)}, f32[8,2,32]{2,1,0:T(2,128)S(1)}, u32[]{:S(2)}, u32[]{:S(2)}) %collective-permute-start.3) | collective-permute-done | bytes 2080 | tf_op jit(solution)/shard_map/ppermute | solution.py:193
  19.1 2.5 %collective-permute-start.4 = (f32[16,2,32]{2,1,0:T(2,128)S(1)}, f32[16,2,32]{2,1,0:T(2,128)S(1)}, u32[]{:S(2)}, u32[]{:S(2)}) collective-permute-start(f32[16,2,32]{2,1,0:T(2,128)S(1)} %get-tuple-element.34), channel_id=1, source_target_pairs={{0,16},{4,20},{8,24},{12,28},{16,0},{20,4},{24,8},{28,12},{1,17},{... | collective-permute-start | bytes 12296 | tf_op jit(solution)/shard_map/ppermute | solution.py:193
  21.7 0.1 reduce_sum.21
  21.8 0.1 squeeze.9
  21.9 0.9 %collective-permute-done.4 = f32[16,2,32]{2,1,0:T(2,128)S(1)} collective-permute-done((f32[16,2,32]{2,1,0:T(2,128)S(1)}, f32[16,2,32]{2,1,0:T(2,128)S(1)}, u32[]{:S(2)}, u32[]{:S(2)}) %collective-permute-start.4) | collective-permute-done | bytes 4128 | tf_op jit(solution)/shard_map/ppermute | solution.py:193
  22.8 0.9 %select_reduce_fusion = f32[2,32]{1,0:T(2,128)S(1)} fusion(f32[32,32]{1,0:T(8,128)S(1)} %bitcast.41, f32[32,32]{1,0:T(8,128)S(1)} %bitcast.40, f32[2,32]{1,0:T(2,128)S(1)} %bitcast.43), kind=kLoop, calls=%fused_computation | loop fusion | flops 196544 | bytes 8704 | tf_op jit(solution)/shard_map/reduce_sum | solution.py:240
  23.7 0.1 max.12
  23.8 0.0 collective-permute-done.6.rest_3_
  23.8 0.0 collective-permute-done.5.rest_2_
  23.8 2.1 %bins_sent.1 = (bf16[16,128,128]{2,1,0:T(8,128)(2,1)S(1)}, bf16[16,128,128]{2,1,0:T(8,128)(2,1)S(1)}) custom-call(s32[8,16]{1,0:T(8,128)S(1)} %get-tuple-element.39.bins_ref, f32[4,16]{1,0:T(4,128)S(1)} %multiply_divide_fusion.scale_ref, bf16[16,128,128]{2,1,0:T(8,128)(2,1)S(1)} %get-tuple-element.12.rest_0_, bf16[16,128,128]{2,1,0:T(8,128)(2,1)S(1)} %match_blocks.3.rest_1_, ...), custom_call_target="tpu_custom_call" | custom-call | flops 6291456 | bytes 3145728 | tf_op jit(solution)/shard_map/bins_sent/pallas_call | solution.py:145
  25.9 1.3 %collective-permute-start.7 = (bf16[16,128,128]{2,1,0:T(8,128)(2,1)S(1)}, bf16[16,128,128]{2,1,0:T(8,128)(2,1)S(1)}, u32[]{:S(2)}, u32[]{:S(2)}) collective-permute-start(bf16[16,128,128]{2,1,0:T(8,128)(2,1)S(1)} %get-tuple-element.16), channel_id=1, source_target_pairs={{0,2},{1,3},{2,0},{3,1},{4,6},{5,7},{6,4},{7,5},{8,10},{9,11},{10,... | collective-permute-start | bytes 1572872 | tf_op jit(solution)/shard_map/ppermute | solution.py:193
  27.3 1.2 %collective-permute-start.9 = (bf16[16,128,128]{2,1,0:T(8,128)(2,1)S(1)}, bf16[16,128,128]{2,1,0:T(8,128)(2,1)S(1)}, u32[]{:S(2)}, u32[]{:S(2)}) collective-permute-start(bf16[16,128,128]{2,1,0:T(8,128)(2,1)S(1)} %get-tuple-element.18), channel_id=1, source_target_pairs={{0,4},{4,0},{8,12},{12,8},{16,20},{20,16},{24,28},{28,24},{1,5},{5... | collective-permute-start | bytes 1572872 | tf_op jit(solution)/shard_map/ppermute | solution.py:193
  28.5 2.1 %bins_kept.1 = (bf16[16,128,128]{2,1,0:T(8,128)(2,1)S(1)}, bf16[16,128,128]{2,1,0:T(8,128)(2,1)S(1)}) custom-call(s32[8,16]{1,0:T(8,128)S(1)} %get-tuple-element.38.bins_ref, f32[4,16]{1,0:T(4,128)S(1)} %multiply_divide_fusion.scale_ref, bf16[16,128,128]{2,1,0:T(8,128)(2,1)S(1)} %get-tuple-element.12.rest_0_, bf16[16,128,128]{2,1,0:T(8,128)(2,1)S(1)} %match_blocks.3.rest_1_, ...), custom_call_target="tpu_custom_call" | custom-call | flops 6291456 | bytes 3145728 | tf_op jit(solution)/shard_map/bins_kept/pallas_call | solution.py:145
  30.6 4.5 %collective-permute-done.7 = bf16[16,128,128]{2,1,0:T(8,128)(2,1)S(1)} collective-permute-done((bf16[16,128,128]{2,1,0:T(8,128)(2,1)S(1)}, bf16[16,128,128]{2,1,0:T(8,128)(2,1)S(1)}, u32[]{:S(2)}, u32[]{:S(2)}) %collective-permute-start.7) | collective-permute-done | bytes 524320 | tf_op jit(solution)/shard_map/ppermute | solution.py:193
  35.0 0.1 add_convert_fusion.1
  35.1 1.0 %collective-permute-start.8 = (bf16[8,128,128]{2,1,0:T(8,128)(2,1)S(1)}, bf16[8,128,128]{2,1,0:T(8,128)(2,1)S(1)}, u32[]{:S(2)}, u32[]{:S(2)}) collective-permute-start(bf16[8,128,128]{2,1,0:T(8,128)(2,1)S(1)} %add_convert_fusion.1), channel_id=1, source_target_pairs={{0,4},{4,0},{8,12},{12,8},{16,20},{20,16},{24,28},{28,24},{1,5},{5... | collective-permute-start | bytes 786440 | tf_op jit(solution)/shard_map/ppermute | solution.py:193
  36.1 0.0 collective-permute-done.9
  36.2 0.1 add_convert_fusion
  36.2 1.2 %collective-permute-start.10 = (bf16[8,128,128]{2,1,0:T(8,128)(2,1)S(1)}, bf16[8,128,128]{2,1,0:T(8,128)(2,1)S(1)}, u32[]{:S(2)}, u32[]{:S(2)}) collective-permute-start(bf16[8,128,128]{2,1,0:T(8,128)(2,1)S(1)} %add_convert_fusion), channel_id=1, source_target_pairs={{0,2},{1,3},{2,0},{3,1},{4,6},{5,7},{6,4},{7,5},{8,10},{9,11},{10,... | collective-permute-start | bytes 786440 | tf_op jit(solution)/shard_map/ppermute | solution.py:193
  37.5 6.1 %collective-permute-done.8 = bf16[8,128,128]{2,1,0:T(8,128)(2,1)S(1)} collective-permute-done((bf16[8,128,128]{2,1,0:T(8,128)(2,1)S(1)}, bf16[8,128,128]{2,1,0:T(8,128)(2,1)S(1)}, u32[]{:S(2)}, u32[]{:S(2)}) %collective-permute-start.8) | collective-permute-done | bytes 262176 | tf_op jit(solution)/shard_map/ppermute | solution.py:193
  43.6 0.1 add_convert_fusion.3
  43.6 0.0 copy-start.4
  43.6 0.0 collective-permute-done.10
  43.7 0.1 add_convert_fusion.2
  43.8 1.2 %collective-permute-start.11 = (bf16[2,4,128,128]{3,2,1,0:T(8,128)(2,1)S(1)}, bf16[2,4,128,128]{3,2,1,0:T(8,128)(2,1)S(1)}, u32[]{:S(2)}, u32[]{:S(2)}) collective-permute-start(bf16[2,4,128,128]{3,2,1,0:T(8,128)(2,1)S(1)} %pad_maximum_fusion), channel_id=1, source_target_pairs={{0,8},{4,12},{8,0},{12,4},{16,24},{20,28},{24,16},{28,20},{1,9},{5... | collective-permute-start | bytes 786440 | tf_op jit(solution)/shard_map/ppermute | solution.py:193
  45.0 0.1 add_bitcast_fusion.2
  45.1 4.3 %collective-permute-done.11 = bf16[2,4,128,128]{3,2,1,0:T(8,128)(2,1)S(1)} collective-permute-done((bf16[2,4,128,128]{3,2,1,0:T(8,128)(2,1)S(1)}, bf16[2,4,128,128]{3,2,1,0:T(8,128)(2,1)S(1)}, u32[]{:S(2)}, u32[]{:S(2)}) %collective-permute-start.11) | collective-permute-done | bytes 262176 | tf_op jit(solution)/shard_map/ppermute | solution.py:193
  49.4 2.2 %collective-permute-start.12 = (bf16[1,4,128,128]{3,2,1,0:T(8,128)(2,1)S(1)}, bf16[1,4,128,128]{3,2,1,0:T(8,128)(2,1)S(1)}, u32[]{:S(2)}, u32[]{:S(2)}) collective-permute-start(bf16[1,4,128,128]{3,2,1,0:T(8,128)(2,1)S(1)} %fusion.1), channel_id=1, source_target_pairs={{0,16},{4,20},{8,24},{12,28},{16,0},{20,4},{24,8},{28,12},{1,17},{... | collective-permute-start | bytes 393224 | tf_op jit(solution)/shard_map/ppermute | solution.py:193
  51.5 4.1 %collective-permute-done.12 = bf16[1,4,128,128]{3,2,1,0:T(8,128)(2,1)S(1)} collective-permute-done((bf16[1,4,128,128]{3,2,1,0:T(8,128)(2,1)S(1)}, bf16[1,4,128,128]{3,2,1,0:T(8,128)(2,1)S(1)}, u32[]{:S(2)}, u32[]{:S(2)}) %collective-permute-start.12) | collective-permute-done | bytes 131104 | tf_op jit(solution)/shard_map/ppermute | solution.py:193
  55.7 0.1 fusion.2.mid_ref
  55.7 10.4 %collective-permute-start.13 = (bf16[4,32,128]{2,1,0:T(8,128)(2,1)S(1)}, bf16[4,32,128]{2,1,0:T(8,128)(2,1)S(1)}, u32[]{:S(2)}, u32[]{:S(2)}) collective-permute-start(bf16[4,32,128]{2,1,0:T(8,128)(2,1)S(1)} %get-tuple-element.31), channel_id=1, source_target_pairs={{0,1},{1,2},{2,3},{4,5},{5,6},{6,7},{8,9},{9,10},{10,11},{12,13},{... | collective-permute-start | bytes 98312 | tf_op jit(solution)/shard_map/ppermute | solution.py:312
  66.2 1.9 %collective-permute-start.14 = (bf16[4,32,128]{2,1,0:T(8,128)(2,1)S(1)}, bf16[4,32,128]{2,1,0:T(8,128)(2,1)S(1)}, u32[]{:S(2)}, u32[]{:S(2)}) collective-permute-start(bf16[4,32,128]{2,1,0:T(8,128)(2,1)S(1)} %get-tuple-element.30), channel_id=1, source_target_pairs={{1,0},{2,1},{3,2},{5,4},{6,5},{7,6},{9,8},{10,9},{11,10},{13,12},{... | collective-permute-start | bytes 98312 | tf_op jit(solution)/shard_map/ppermute | solution.py:313
  68.1 0.0 copy-done.4
  68.1 0.0 collective-permute-done.13.low_ref
  68.2 3.3 %collective-permute-done.14.high_ref = bf16[4,32,128]{2,1,0:T(8,128)(2,1)S(1)} collective-permute-done((bf16[4,32,128]{2,1,0:T(8,128)(2,1)S(1)}, bf16[4,32,128]{2,1,0:T(8,128)(2,1)S(1)}, u32[]{:S(2)}, u32[]{:S(2)}) %collective-permute-start.14) | collective-permute-done | bytes 32800 | tf_op jit(solution)/shard_map/ppermute | solution.py:313
  71.4 1.4 %detect.1 = f32[128,512]{1,0:T(8,128)} custom-call(f32[1,41]{1,0:T(1,128)S(1)} %bitcast_convert_fusion.1.taps_ref, bf16[4,128,128]{2,1,0:T(8,128)(2,1)S(1)} %fusion.2.mid_ref, bf16[4,32,128]{2,1,0:T(8,128)(2,1)S(1)} %collective-permute-done.13.low_ref, bf16[4,32,128]{2,1,0:T(8,128)(2,1)S(1)} %collective-permute-done.14.high_ref), custom_call_target="tpu_custom_call" | custom-call | tf_op jit(solution)/shard_map/detect/pallas_call | solution.py:181
  (24 shorter events, 0.4 us)
Async XLA Ops:
  1.4 8.9 %collective-permute-start = (f32[1,2,32]{2,1,0:T(2,128)S(1)}, f32[1,2,32]{2,1,0:T(2,128)S(1)}, u32[]{:S(2)}, u32[]{:S(2)}) collective-permute-start(f32[1,2,32]{2,1,0:T(2,128)S(1)} %maximum_bitcast_fusion), channel_id=1, source_target_pairs={{0,1},{1,0},{2,3},{3,2},{4,5},{5,4},{6,7},{7,6},{8,9},{9,8},{10,11... | collective-permute-start | bytes 776 | tf_op jit(solution)/shard_map/ppermute | solution.py:193
  2.3 1.5 %copy-start = (bf16[168,5376]{1,0:T(8,128)(2,1)S(1)}, bf16[168,5376]{1,0:T(8,128)(2,1)}, u32[]{:S(2)}) copy-start(bf16[168,5376]{1,0:T(8,128)(2,1)} %raw_ref.3) | copy-start | bytes 5419012
  3.7 0.7 copy-start.1
  4.4 0.7 copy-start.2
  7.5 5.7 %copy-start.3 = (f32[6]{0:T(128)S(1)}, f32[6]{0:T(128)}, u32[]{:S(2)}) copy-start(f32[6]{0:T(128)} %param.18) | copy-start | bytes 76
  9.7 14.1 %collective-permute-start.6 = (bf16[16,128,128]{2,1,0:T(8,128)(2,1)S(1)}, bf16[16,128,128]{2,1,0:T(8,128)(2,1)S(1)}, u32[]{:S(2)}, u32[]{:S(2)}) collective-permute-start(bf16[16,128,128]{2,1,0:T(8,128)(2,1)S(1)} %match_blocks.3.rest_1_), channel_id=1, source_target_pairs={{0,1},{1,0},{2,3},{3,2},{4,5},{5,4},{6,7},{7,6},{8,9},{9,8},{10,11... | collective-permute-start | bytes 1572872 | tf_op jit(solution)/shard_map/ppermute | solution.py:193
  10.2 13.6 %collective-permute-start.5 = (bf16[16,128,128]{2,1,0:T(8,128)(2,1)S(1)}, bf16[16,128,128]{2,1,0:T(8,128)(2,1)S(1)}, u32[]{:S(2)}, u32[]{:S(2)}) collective-permute-start(bf16[16,128,128]{2,1,0:T(8,128)(2,1)S(1)} %get-tuple-element.12.rest_0_), channel_id=1, source_target_pairs={{0,1},{1,0},{2,3},{3,2},{4,5},{5,4},{6,7},{7,6},{8,9},{9,8},{10,11... | collective-permute-start | bytes 1572872 | tf_op jit(solution)/shard_map/ppermute | solution.py:193
  10.3 3.7 %collective-permute-start.1 = (f32[2,2,32]{2,1,0:T(2,128)S(1)}, f32[2,2,32]{2,1,0:T(2,128)S(1)}, u32[]{:S(2)}, u32[]{:S(2)}) collective-permute-start(f32[2,2,32]{2,1,0:T(2,128)S(1)} %pad_maximum_fusion.3), channel_id=1, source_target_pairs={{0,2},{1,3},{2,0},{3,1},{4,6},{5,7},{6,4},{7,5},{8,10},{9,11},{10,... | collective-permute-start | bytes 1544 | tf_op jit(solution)/shard_map/ppermute | solution.py:193
  14.0 2.5 %collective-permute-start.2 = (f32[4,2,32]{2,1,0:T(2,128)S(1)}, f32[4,2,32]{2,1,0:T(2,128)S(1)}, u32[]{:S(2)}, u32[]{:S(2)}) collective-permute-start(f32[4,2,32]{2,1,0:T(2,128)S(1)} %pad_maximum_fusion.2), channel_id=1, source_target_pairs={{0,4},{4,0},{8,12},{12,8},{16,20},{20,16},{24,28},{28,24},{1,5},{5... | collective-permute-start | bytes 3080 | tf_op jit(solution)/shard_map/ppermute | solution.py:193
  16.5 2.6 %collective-permute-start.3 = (f32[8,2,32]{2,1,0:T(2,128)S(1)}, f32[8,2,32]{2,1,0:T(2,128)S(1)}, u32[]{:S(2)}, u32[]{:S(2)}) collective-permute-start(f32[8,2,32]{2,1,0:T(2,128)S(1)} %pad_maximum_fusion.1), channel_id=1, source_target_pairs={{0,8},{4,12},{8,0},{12,4},{16,24},{20,28},{24,16},{28,20},{1,9},{5... | collective-permute-start | bytes 6152 | tf_op jit(solution)/shard_map/ppermute | solution.py:193
  19.1 3.7 %collective-permute-start.4 = (f32[16,2,32]{2,1,0:T(2,128)S(1)}, f32[16,2,32]{2,1,0:T(2,128)S(1)}, u32[]{:S(2)}, u32[]{:S(2)}) collective-permute-start(f32[16,2,32]{2,1,0:T(2,128)S(1)} %get-tuple-element.34), channel_id=1, source_target_pairs={{0,16},{4,20},{8,24},{12,28},{16,0},{20,4},{24,8},{28,12},{1,17},{... | collective-permute-start | bytes 12296 | tf_op jit(solution)/shard_map/ppermute | solution.py:193
  25.9 9.1 %collective-permute-start.7 = (bf16[16,128,128]{2,1,0:T(8,128)(2,1)S(1)}, bf16[16,128,128]{2,1,0:T(8,128)(2,1)S(1)}, u32[]{:S(2)}, u32[]{:S(2)}) collective-permute-start(bf16[16,128,128]{2,1,0:T(8,128)(2,1)S(1)} %get-tuple-element.16), channel_id=1, source_target_pairs={{0,2},{1,3},{2,0},{3,1},{4,6},{5,7},{6,4},{7,5},{8,10},{9,11},{10,... | collective-permute-start | bytes 1572872 | tf_op jit(solution)/shard_map/ppermute | solution.py:193
  27.3 8.9 %collective-permute-start.9 = (bf16[16,128,128]{2,1,0:T(8,128)(2,1)S(1)}, bf16[16,128,128]{2,1,0:T(8,128)(2,1)S(1)}, u32[]{:S(2)}, u32[]{:S(2)}) collective-permute-start(bf16[16,128,128]{2,1,0:T(8,128)(2,1)S(1)} %get-tuple-element.18), channel_id=1, source_target_pairs={{0,4},{4,0},{8,12},{12,8},{16,20},{20,16},{24,28},{28,24},{1,5},{5... | collective-permute-start | bytes 1572872 | tf_op jit(solution)/shard_map/ppermute | solution.py:193
  35.1 8.5 %collective-permute-start.8 = (bf16[8,128,128]{2,1,0:T(8,128)(2,1)S(1)}, bf16[8,128,128]{2,1,0:T(8,128)(2,1)S(1)}, u32[]{:S(2)}, u32[]{:S(2)}) collective-permute-start(bf16[8,128,128]{2,1,0:T(8,128)(2,1)S(1)} %add_convert_fusion.1), channel_id=1, source_target_pairs={{0,4},{4,0},{8,12},{12,8},{16,20},{20,16},{24,28},{28,24},{1,5},{5... | collective-permute-start | bytes 786440 | tf_op jit(solution)/shard_map/ppermute | solution.py:193
  36.2 7.4 %collective-permute-start.10 = (bf16[8,128,128]{2,1,0:T(8,128)(2,1)S(1)}, bf16[8,128,128]{2,1,0:T(8,128)(2,1)S(1)}, u32[]{:S(2)}, u32[]{:S(2)}) collective-permute-start(bf16[8,128,128]{2,1,0:T(8,128)(2,1)S(1)} %add_convert_fusion), channel_id=1, source_target_pairs={{0,2},{1,3},{2,0},{3,1},{4,6},{5,7},{6,4},{7,5},{8,10},{9,11},{10,... | collective-permute-start | bytes 786440 | tf_op jit(solution)/shard_map/ppermute | solution.py:193
  43.6 24.5 %copy-start.4 = (f32[41]{0:T(128)S(1)}, f32[41]{0:T(128)}, u32[]{:S(2)}) copy-start(f32[41]{0:T(128)} %param.19) | copy-start | bytes 496
  43.8 5.6 %collective-permute-start.11 = (bf16[2,4,128,128]{3,2,1,0:T(8,128)(2,1)S(1)}, bf16[2,4,128,128]{3,2,1,0:T(8,128)(2,1)S(1)}, u32[]{:S(2)}, u32[]{:S(2)}) collective-permute-start(bf16[2,4,128,128]{3,2,1,0:T(8,128)(2,1)S(1)} %pad_maximum_fusion), channel_id=1, source_target_pairs={{0,8},{4,12},{8,0},{12,4},{16,24},{20,28},{24,16},{28,20},{1,9},{5... | collective-permute-start | bytes 786440 | tf_op jit(solution)/shard_map/ppermute | solution.py:193
  49.4 6.3 %collective-permute-start.12 = (bf16[1,4,128,128]{3,2,1,0:T(8,128)(2,1)S(1)}, bf16[1,4,128,128]{3,2,1,0:T(8,128)(2,1)S(1)}, u32[]{:S(2)}, u32[]{:S(2)}) collective-permute-start(bf16[1,4,128,128]{3,2,1,0:T(8,128)(2,1)S(1)} %fusion.1), channel_id=1, source_target_pairs={{0,16},{4,20},{8,24},{12,28},{16,0},{20,4},{24,8},{28,12},{1,17},{... | collective-permute-start | bytes 393224 | tf_op jit(solution)/shard_map/ppermute | solution.py:193
  55.7 12.4 %collective-permute-start.13 = (bf16[4,32,128]{2,1,0:T(8,128)(2,1)S(1)}, bf16[4,32,128]{2,1,0:T(8,128)(2,1)S(1)}, u32[]{:S(2)}, u32[]{:S(2)}) collective-permute-start(bf16[4,32,128]{2,1,0:T(8,128)(2,1)S(1)} %get-tuple-element.31), channel_id=1, source_target_pairs={{0,1},{1,2},{2,3},{4,5},{5,6},{6,7},{8,9},{9,10},{10,11},{12,13},{... | collective-permute-start | bytes 98312 | tf_op jit(solution)/shard_map/ppermute | solution.py:312
  66.2 5.2 %collective-permute-start.14 = (bf16[4,32,128]{2,1,0:T(8,128)(2,1)S(1)}, bf16[4,32,128]{2,1,0:T(8,128)(2,1)S(1)}, u32[]{:S(2)}, u32[]{:S(2)}) collective-permute-start(bf16[4,32,128]{2,1,0:T(8,128)(2,1)S(1)} %get-tuple-element.30), channel_id=1, source_target_pairs={{1,0},{2,1},{3,2},{5,4},{6,5},{7,6},{9,8},{10,9},{11,10},{13,12},{... | collective-permute-start | bytes 98312 | tf_op jit(solution)/shard_map/ppermute | solution.py:313

commit v3 on v1

--- a/solution.py
+++ b/solution.py
@@ -31,24 +31,27 @@
     return jnp.concatenate(parts, axis=1)
 
 
-def match_kernel(coef_ref, raw_ref, row_ref, col_ref, out_ref, rowk_ref, colk_ref):
+def match_kernel(small_ref, raw_ref, out_ref, rowk_ref, colk_ref):
     margin_side = raw_ref.shape[0]
-    basis_count = row_ref.shape[0]
-    block_count, block_side, unused = out_ref.shape
+    basis_count = small_ref.shape[0] // 3
+    count, block_side, unused = out_ref.shape
+    tap_count = margin_side - block_side + 1
     width = colk_ref.shape[0] // basis_count
     for k in range(basis_count):
-        rows = banded(lanes_at(row_ref[k : k + 1, :], 0, width), block_side, width)
+        rows = banded(lanes_at(small_ref[k : k + 1, :tap_count], 0, width), block_side, width)
         rowk_ref[k * block_side : (k + 1) * block_side, :] = rows[:, :margin_side].astype(jnp.bfloat16)
-        cols = banded(lanes_at(col_ref[k : k + 1, :], 0, width), block_side, width)
+        place = basis_count + k
+        cols = banded(lanes_at(small_ref[place : place + 1, :tap_count], 0, width), block_side, width)
         colk_ref[k * width : (k + 1) * width, :] = cols.T.astype(jnp.bfloat16)
-    for n in range(block_count):
+    for n in range(count):
         block = raw_ref[:, n * margin_side : (n + 1) * margin_side]
         sectioned = jnp.dot(rowk_ref[...], block, preferred_element_type=jnp.float32)
         total = None
         for k in range(basis_count):
-            part = (sectioned[k * block_side : (k + 1) * block_side] * coef_ref[n, k]).astype(jnp.bfloat16)
+            place = 2 * basis_count + k
+            part = sectioned[k * block_side : (k + 1) * block_side] * small_ref[place : place + 1, n : n + 1]
             term = jnp.dot(
-                part,
+                part.astype(jnp.bfloat16),
                 colk_ref[k * width : k * width + margin_side, :],
                 preferred_element_type=jnp.float32,
             )
@@ -56,74 +59,69 @@
         out_ref[n] = total.astype(jnp.bfloat16)
 
 
-def match_blocks(raw_blocks, coef, row_basis, col_basis, block_side):
-    margin_side = raw_blocks.shape[0]
-    block_count = raw_blocks.shape[1] // margin_side
-    basis_count = row_basis.shape[0]
+def match_blocks(small, raw, block_side):
+    margin_side = raw.shape[0]
+    count = raw.shape[1] // margin_side
+    basis_count = small.shape[0] // 3
     width = up(margin_side, 128)
-    flops = 2 * block_count * basis_count * block_side * margin_side * (margin_side + block_side)
+    flops = 2 * count * basis_count * block_side * margin_side * (margin_side + block_side)
     return pl.pallas_call(
         match_kernel,
-        out_shape=jax.ShapeDtypeStruct((block_count, block_side, block_side), jnp.bfloat16),
-        in_specs=[
-            pl.BlockSpec(memory_space=SMEM),
-            pl.BlockSpec(memory_space=VMEM),
-            pl.BlockSpec(memory_space=VMEM),
-            pl.BlockSpec(memory_space=VMEM),
-        ],
+        out_shape=jax.ShapeDtypeStruct((count, block_side, block_side), jnp.bfloat16),
+        in_specs=[pl.BlockSpec(memory_space=VMEM)] * 2,
         out_specs=pl.BlockSpec(memory_space=VMEM),
         scratch_shapes=[
             VMEM((basis_count * block_side, margin_side), jnp.bfloat16),
             VMEM((basis_count * width, block_side), jnp.bfloat16),
         ],
-        compiler_params=pltpu.CompilerParams(vmem_limit_bytes=32 << 20),
-        cost_estimate=pl.CostEstimate(flops=2 * flops, bytes_accessed=4 << 20, transcendentals=0),
+        compiler_params=pltpu.CompilerParams(vmem_limit_bytes=12 << 20),
+        cost_estimate=pl.CostEstimate(flops=4 * flops, bytes_accessed=4 << 20, transcendentals=0),
         name="match_blocks",
-    )(coef, raw_blocks, row_basis, col_basis)
-
-
-def bin_kernel(bins_ref, scale_ref, own_ref, other_ref, *rest):
-    outs, acc_ref = rest[:-1], rest[-1]
-    step = outs[0].shape[0]
-    chunk = pl.program_id(0)
+    )(small, raw)
+
+
+def bin_kernel(bins_ref, scale_ref, *rest):
+    (own_ref, other_ref), outs, acc_ref = rest[:2], rest[2:-1], rest[-1]
+    size = outs[0].shape[0]
+    step = acc_ref.shape[0]
+    low = pl.program_id(0) * step
     acc_ref[...] = jnp.zeros_like(acc_ref)
     for source, blocks_ref in enumerate((own_ref, other_ref)):
-
-        def add(n, carry, source=source, blocks_ref=blocks_ref):
-            place = bins_ref[source, n] - chunk * step
-            group = bins_ref[source + 2, n]
-
-            @pl.when((place >= 0) & (place < step) & (group >= 0))
-            def _():
-                slot = group * step + place
+        for n in range(blocks_ref.shape[0]):
+            slot = bins_ref[source, n] - low
+
+            @pl.when((slot >= 0) & (slot < step))
+            def _(source=source, blocks_ref=blocks_ref, n=n, slot=slot):
                 acc_ref[slot] += scale_ref[source, n] * blocks_ref[n].astype(jnp.float32)
 
-            return carry
-
-        lax.fori_loop(0, blocks_ref.shape[0], add, 0)
     for index, out_ref in enumerate(outs):
-        out_ref[...] = acc_ref[index * step : (index + 1) * step].astype(out_ref.dtype)
+        out_ref[...] = acc_ref[index * size : (index + 1) * size].astype(out_ref.dtype)
 
 
 def bin_blocks(bins, scale, own, other, groups, size, name):
     block_side = own.shape[1]
-    step = min(size, 16)
+    if groups * size > 64:
+        groups, size, split = 1, groups * size, groups
+    else:
+        split = 1
+    step = min(groups * size, 64)
     whole = pl.BlockSpec(own.shape, lambda g: (0, 0, 0))
-    part = pl.BlockSpec((step, block_side, block_side), lambda g: (g, 0, 0))
-    shape = jax.ShapeDtypeStruct((size, block_side, block_side), jnp.bfloat16)
-    return pl.pallas_call(
+    part = pl.BlockSpec((step // groups, block_side, block_side), lambda g: (g, 0, 0))
+    moved = 4 * own.size + 2 * groups * size * block_side**2
+    found = pl.pallas_call(
         bin_kernel,
-        grid=(size // step,),
-        out_shape=[shape] * groups,
+        grid=(groups * size // step,),
+        out_shape=[jax.ShapeDtypeStruct((size, block_side, block_side), jnp.bfloat16)] * groups,
         in_specs=[pl.BlockSpec(memory_space=SMEM), pl.BlockSpec(memory_space=SMEM), whole, whole],
         out_specs=[part] * groups,
-        scratch_shapes=[VMEM((groups * step, block_side, block_side), jnp.float32)],
-        compiler_params=pltpu.CompilerParams(vmem_limit_bytes=40 << 20),
-        cost_estimate=pl.CostEstimate(
-            flops=4 * own.size, bytes_accessed=4 * own.size + 2 * groups * size * block_side**2, transcendentals=0
-        ),
+        scratch_shapes=[VMEM((step, block_side, block_side), jnp.float32)],
+        compiler_params=pltpu.CompilerParams(vmem_limit_bytes=20 << 20),
+        cost_estimate=pl.CostEstimate(flops=2 * moved, bytes_accessed=moved, transcendentals=0),
         name=name,
     )(bins, scale, own, other)
+    if split > 1:
+        found = jnp.split(found[0], split)
+    return found
 
 
 def filter_kernel(taps_ref, mid_ref, low_ref, high_ref, out_ref):
@@ -154,7 +152,7 @@
         out_shape=jax.ShapeDtypeStruct((side, cells * side), jnp.float32),
         in_specs=[pl.BlockSpec(memory_space=VMEM)] * 4,
         out_specs=pl.BlockSpec(memory_space=VMEM),
-        compiler_params=pltpu.CompilerParams(vmem_limit_bytes=32 << 20),
+        compiler_params=pltpu.CompilerParams(vmem_limit_bytes=12 << 20),
         name="detect",
     )(taps, mid, low, high)
 
@@ -168,8 +166,7 @@
     total = None
     for part in parts:
         half = part.shape[0] // 2
-        piece = part[half:] if send else part[:half]
-        piece = piece.astype(jnp.float32)
+        piece = (part[half:] if send else part[:half]).astype(jnp.float32)
         total = piece if total is None else total + piece
     return total
 
@@ -199,17 +196,18 @@
 
     key = (patch_of_block[:, 0] * BANDS + band_of_block) * CELLS + cell_of_block
     facts = jnp.stack([key.astype(jnp.float32), block_weight.astype(jnp.float32)])
-    all_facts = lax.all_gather(facts, ("sky", "band"), axis=0)
-
-    matched = match_blocks(raw_blocks, basis_coef.astype(jnp.float32), row_basis, col_basis, block_side)
+    chip_facts = jnp.concatenate(
+        [facts]
+        + [lax.ppermute(facts, "band", [(i, i ^ off) for i in range(band_count)]) for off in range(1, band_count)]
+    )
+    small = [row_basis, col_basis, basis_coef.T.astype(jnp.float32)]
+    lanes = max(part.shape[1] for part in small)
+    small = jnp.concatenate([jnp.pad(part, ((0, 0), (0, lanes - part.shape[1]))) for part in small])
+    matched = match_blocks(small, raw_blocks, block_side)
     from_pair = swap(matched, "band", 0)
-
-    here = sky_here * band_count + band_here
-    pair = jnp.stack([here, here ^ 1])
-    near = jnp.concatenate(
-        [lax.dynamic_slice_in_dim(all_facts, here, 1, 0), lax.dynamic_slice_in_dim(all_facts, here ^ 1, 1, 0)]
-    )
-    near_key, near_weight = near[:, 0], near[:, 1]
+    all_facts = lax.all_gather(chip_facts, "sky", axis=0, tiled=True).reshape(-1, 2, block_count)
+
+    near_key, near_weight = (chip_facts[:4].reshape(2, 2, block_count)[:, i] for i in range(2))
     same = near_key[:, :, None, None] == all_facts[None, None, :, 0]
     weight_sum = jnp.sum(jnp.where(same, all_facts[None, None, :, 1], 0.0), axis=(2, 3))
     near_key = near_key.astype(jnp.int32)
@@ -240,9 +238,9 @@
     sent = place >= size
     place = place % size
     group = second.astype(jnp.int32)
-    sent_bins = jnp.concatenate([place, jnp.where(mine & sent, group, -1)])
-    kept_bins = jnp.concatenate([place, jnp.where(mine & ~sent, group, -1)])
-
+    place = group * size + place
+    sent_bins = jnp.where(mine & sent, place, -1)
+    kept_bins = jnp.where(mine & ~sent, place, -1)
     send_a, send_b = bin_blocks(sent_bins, scale, matched, from_pair, 2, size, "bins_sent")
     steps_a = [("band", bit) for bit in range(1, band_bits)] + [("sky", 0)]
     steps_b = [("sky", 0)] + [("band", bit) for bit in range(1, band_bits)]

time: 101 us -> 89.8 us (0.89)
  blocking collectives: 43.1 us -> 24.6 us
  starting transfers between devices: 9.55 us -> 24.8 us
  waiting for transfers between devices: 32.3 us -> 25.6 us
  other arithmetic: 1.51 us -> 4.22 us
  local copies, waits for them, and re-layouts: 3.68 us -> 1.56 us
  Pallas kernels: 10 us -> 8.51 us
    all_gather x1, blocking collectives: 43.1 us -> 24.6 us  [local(): lax.all_gather(chip_facts, 'sky', axis=0, tiled=True)]
    ppermute x1, starting transfers between devices: 6.11 us -> 14.3 us  [local(): low = lax.ppermute(combined[:, block_side - edge:], 'band', forward)]
    ppermute x7, waiting for transfers between devices: 29 us -> 22.4 us  [swap(): return lax.ppermute(array, axis, [(i, i ^ 1 << bit) for i in range(count)])]
    ppermute x7, starting transfers between devices: 1.52 us -> 5.73 us  [swap(): return lax.ppermute(array, axis, [(i, i ^ 1 << bit) for i in range(count)])]
    ppermute x0 -> x3, starting transfers between devices: none -> 2.86 us  [local(): lax.ppermute(facts, 'band', [(i, i ^ off) for i in range(band_count)])]
    pallas_call x3, Pallas kernels: 8.66 us -> 7.13 us  [the longest x1 4.21 us: match_blocks(): pl.pallas_call(match_kernel, out_shape=jax.ShapeDtypeStruct((count, block...]
    unnamed x18 -> x6, local copies, waits for them, and re-layouts: 2.88 us -> 1.5 us
    another operation x2 -> x3, other arithmetic: 0.01 us -> 1.36 us  [local(): jnp.stack([key.astype(jnp.float32), block_weight.astype(jnp.float32)])]
  transfers between devices with their start and end apart: 9 -> 12, of which waited for: 6 -> 6; matrix products, arithmetic and copies ran while one was open for 1% -> 3% of each run, Pallas kernels for 2% -> 6%
where the time goes in v3:
time: 89.8 us; the launch traced here: 89.5 us
  waiting for transfers between devices  25.6 us (29%)
  starting transfers between devices  24.8 us (28%)
  blocking collectives  24.6 us (27%)
  Pallas kernels  8.51 us (9%)
  other arithmetic  4.22 us (5%)
  local copies, waits for them, and re-layouts  1.56 us (2%)
    all_gather x1, blocking collectives, local(): lax.all_gather(chip_facts, 'sky', axis=0, tiled=True)  24.6 us
    ppermute x7, waiting for transfers between devices, swap(): return lax.ppermute(array, axis, [(i, i ^ 1 << bit) for i in range(count)])  22.4 us
    ppermute x1, starting transfers between devices, local(): low = lax.ppermute(combined[:, block_side - edge:], 'band', forward)  14.3 us
    ppermute x7, starting transfers between devices, swap(): return lax.ppermute(array, axis, [(i, i ^ 1 << bit) for i in range(count)])  5.73 us
    pallas_call x1, Pallas kernels, match_blocks(): pl.pallas_call(match_kernel, out_shape=jax.ShapeDtypeStruct((count, block...  4.21 us
    ppermute x1, waiting for transfers between devices, local(): high = lax.ppermute(combined[:, :edge], 'band', backward)  3.27 us
    pallas_call x2, Pallas kernels, bin_blocks(): pl.pallas_call(bin_kernel, grid=(groups * size // step,), out_shape=[jax....  2.92 us
    ppermute x3, starting transfers between devices, local(): lax.ppermute(facts, 'band', [(i, i ^ off) for i in range(band_count)])  2.86 us
  transfers between devices with their start and end apart: 12, of which 6 were waited for; matrix products, arithmetic and copies ran while one was open for 3% of the time, Pallas kernels for 6%

profile of v3, /device:TPU:1, one launch (start us, length us, event | category | flops | bytes accessed | tf_op | source)
XLA Modules:
  0.0 89.5 jit_solution(6066566140458541255)
XLA Ops:
  0.0 0.7 bitcast_convert_fusion.1
  0.7 0.7 convert_bitcast_fusion
  1.4 0.1 collective-permute-start
  1.5 2.7 %collective-permute-start.1 = (f32[2,32]{1,0:T(2,128)S(1)}, f32[2,32]{1,0:T(2,128)S(1)}, u32[]{:S(2)}, u32[]{:S(2)}) collective-permute-start(f32[2,32]{1,0:T(2,128)S(1)} %pad_maximum_fusion.3), channel_id=1, source_target_pairs={{0,2},{1,3},{2,0},{3,1},{4,6},{5,7},{6,4},{7,5},{8,10},{9,11},{10,... | collective-permute-start | bytes 776 | tf_op jit(solution)/shard_map/ppermute | solution.py:201
  4.2 0.0 collective-permute-start.2
  4.2 0.7 pad_convert_fusion
  4.9 0.7 pad_maximum_fusion.1.small_ref
  5.6 0.0 copy-start
  5.6 1.5 %copy-done = bf16[168,5376]{1,0:T(8,128)(2,1)S(1)} copy-done((bf16[168,5376]{1,0:T(8,128)(2,1)S(1)}, bf16[168,5376]{1,0:T(8,128)(2,1)}, u32[]{:S(2)}) %copy-start) | copy-done | bytes 1806360
  7.1 0.0 copy-start.1
  7.1 4.2 %match_blocks.1.rest_0_ = bf16[32,128,128]{2,1,0:T(8,128)(2,1)S(1)} custom-call(f32[9,41]{1,0:T(8,128)S(1)} %pad_maximum_fusion.1.small_ref, bf16[168,5376]{1,0:T(8,128)(2,1)S(1)} %copy-done), custom_call_target="tpu_custom_call" | custom-call | flops 4888461312 | bytes 4194304 | tf_op jit(solution)/shard_map/match_blocks/pallas_call | solution.py:68
  11.3 0.4 collective-permute-start.3
  11.8 0.0 collective-permute-done
  11.8 0.0 collective-permute-done.1
  11.8 0.0 collective-permute-done.2
  11.8 24.6 %all_gather.3 = f32[64,32]{1,0:T(8,128)S(1)} all-gather(f32[8,32]{1,0:T(8,128)S(1)} %concatenate.21), channel_id=1, replica_groups=mesh['sky'=8,'band'=4] {'sky'}, dimensions={0}, use_global_device_ids=true | all-gather | bytes 9216 | tf_op jit(solution)/shard_map/all_gather | solution.py:208
  36.5 0.0 copy-done.1
  36.5 0.1 fusion.3
  36.6 0.9 select_reduce_fusion
  37.5 0.0 collective-permute-done.3.rest_1_
  37.5 1.4 %bins_sent.1 = (bf16[16,128,128]{2,1,0:T(8,128)(2,1)S(1)}, bf16[16,128,128]{2,1,0:T(8,128)(2,1)S(1)}) custom-call(s32[2,32]{1,0:T(2,128)S(1)} %and_select_fusion.bins_ref, f32[2,32]{1,0:T(2,128)S(1)} %maximum_divide_fusion.scale_ref, bf16[32,128,128]{2,1,0:T(8,128)(2,1)S(1)} %match_blocks.1.rest_0_, bf16[32,128,128]{2,1,0:T(8,128)(2,1)S(1)} %collective-permute-done.3.rest_1_), custom_call_target="tpu_custom_call" | custom-call | flops 6291456 | bytes 3145728 | tf_op jit(solution)/shard_map/bins_sent/pallas_call | solution.py:111
  38.9 1.3 %collective-permute-start.4 = (bf16[16,128,128]{2,1,0:T(8,128)(2,1)S(1)}, bf16[16,128,128]{2,1,0:T(8,128)(2,1)S(1)}, u32[]{:S(2)}, u32[]{:S(2)}) collective-permute-start(bf16[16,128,128]{2,1,0:T(8,128)(2,1)S(1)} %get-tuple-element.10), channel_id=1, source_target_pairs={{0,2},{1,3},{2,0},{3,1},{4,6},{5,7},{6,4},{7,5},{8,10},{9,11},{10,... | collective-permute-start | bytes 1572872 | tf_op jit(solution)/shard_map/ppermute | solution.py:162
  40.2 1.2 %collective-permute-start.6 = (bf16[16,128,128]{2,1,0:T(8,128)(2,1)S(1)}, bf16[16,128,128]{2,1,0:T(8,128)(2,1)S(1)}, u32[]{:S(2)}, u32[]{:S(2)}) collective-permute-start(bf16[16,128,128]{2,1,0:T(8,128)(2,1)S(1)} %get-tuple-element.12), channel_id=1, source_target_pairs={{0,4},{4,0},{8,12},{12,8},{16,20},{20,16},{24,28},{28,24},{1,5},{5... | collective-permute-start | bytes 1572872 | tf_op jit(solution)/shard_map/ppermute | solution.py:162
  41.5 1.5 %bins_kept.1 = (bf16[16,128,128]{2,1,0:T(8,128)(2,1)S(1)}, bf16[16,128,128]{2,1,0:T(8,128)(2,1)S(1)}) custom-call(s32[2,32]{1,0:T(2,128)S(1)} %get-tuple-element.13.bins_ref, f32[2,32]{1,0:T(2,128)S(1)} %maximum_divide_fusion.scale_ref, bf16[32,128,128]{2,1,0:T(8,128)(2,1)S(1)} %match_blocks.1.rest_0_, bf16[32,128,128]{2,1,0:T(8,128)(2,1)S(1)} %collective-permute-done.3.rest_1_), custom_call_target="tpu_custom_call" | custom-call | flops 6291456 | bytes 3145728 | tf_op jit(solution)/shard_map/bins_kept/pallas_call | solution.py:111
  42.9 4.1 %collective-permute-done.4 = bf16[16,128,128]{2,1,0:T(8,128)(2,1)S(1)} collective-permute-done((bf16[16,128,128]{2,1,0:T(8,128)(2,1)S(1)}, bf16[16,128,128]{2,1,0:T(8,128)(2,1)S(1)}, u32[]{:S(2)}, u32[]{:S(2)}) %collective-permute-start.4) | collective-permute-done | bytes 524320 | tf_op jit(solution)/shard_map/ppermute | solution.py:162
  47.0 0.1 add_convert_fusion.1
  47.1 1.3 %collective-permute-start.5 = (bf16[8,128,128]{2,1,0:T(8,128)(2,1)S(1)}, bf16[8,128,128]{2,1,0:T(8,128)(2,1)S(1)}, u32[]{:S(2)}, u32[]{:S(2)}) collective-permute-start(bf16[8,128,128]{2,1,0:T(8,128)(2,1)S(1)} %add_convert_fusion.1), channel_id=1, source_target_pairs={{0,4},{4,0},{8,12},{12,8},{16,20},{20,16},{24,28},{28,24},{1,5},{5... | collective-permute-start | bytes 786440 | tf_op jit(solution)/shard_map/ppermute | solution.py:162
  48.4 0.0 collective-permute-done.6
  48.4 0.1 add_convert_fusion
  48.5 1.3 %collective-permute-start.7 = (bf16[8,128,128]{2,1,0:T(8,128)(2,1)S(1)}, bf16[8,128,128]{2,1,0:T(8,128)(2,1)S(1)}, u32[]{:S(2)}, u32[]{:S(2)}) collective-permute-start(bf16[8,128,128]{2,1,0:T(8,128)(2,1)S(1)} %add_convert_fusion), channel_id=1, source_target_pairs={{0,2},{1,3},{2,0},{3,1},{4,6},{5,7},{6,4},{7,5},{8,10},{9,11},{10,... | collective-permute-start | bytes 786440 | tf_op jit(solution)/shard_map/ppermute | solution.py:162
  49.8 5.3 %collective-permute-done.5 = bf16[8,128,128]{2,1,0:T(8,128)(2,1)S(1)} collective-permute-done((bf16[8,128,128]{2,1,0:T(8,128)(2,1)S(1)}, bf16[8,128,128]{2,1,0:T(8,128)(2,1)S(1)}, u32[]{:S(2)}, u32[]{:S(2)}) %collective-permute-start.5) | collective-permute-done | bytes 262176 | tf_op jit(solution)/shard_map/ppermute | solution.py:162
  55.0 0.1 add_convert_fusion.3
  55.1 0.0 copy-start.2
  55.1 1.8 %collective-permute-done.7 = bf16[8,128,128]{2,1,0:T(8,128)(2,1)S(1)} collective-permute-done((bf16[8,128,128]{2,1,0:T(8,128)(2,1)S(1)}, bf16[8,128,128]{2,1,0:T(8,128)(2,1)S(1)}, u32[]{:S(2)}, u32[]{:S(2)}) %collective-permute-start.7) | collective-permute-done | bytes 262176 | tf_op jit(solution)/shard_map/ppermute | solution.py:162
  56.9 0.1 add_convert_fusion.2
  57.0 0.1 collective-permute-start.8
  57.1 0.1 add_bitcast_fusion.3
  57.1 0.1 add_bitcast_fusion.2
  57.2 5.4 %collective-permute-done.8 = bf16[2,4,128,128]{3,2,1,0:T(8,128)(2,1)S(1)} collective-permute-done((bf16[2,4,128,128]{3,2,1,0:T(8,128)(2,1)S(1)}, bf16[2,4,128,128]{3,2,1,0:T(8,128)(2,1)S(1)}, u32[]{:S(2)}, u32[]{:S(2)}) %collective-permute-start.8) | collective-permute-done | bytes 262176 | tf_op jit(solution)/shard_map/ppermute | solution.py:162
  62.6 0.1 collective-permute-start.9
  62.7 5.8 %collective-permute-done.9 = bf16[1,4,128,128]{3,2,1,0:T(8,128)(2,1)S(1)} collective-permute-done((bf16[1,4,128,128]{3,2,1,0:T(8,128)(2,1)S(1)}, bf16[1,4,128,128]{3,2,1,0:T(8,128)(2,1)S(1)}, u32[]{:S(2)}, u32[]{:S(2)}) %collective-permute-start.9) | collective-permute-done | bytes 131104 | tf_op jit(solution)/shard_map/ppermute | solution.py:162
  68.5 0.1 fusion.2.mid_ref
  68.6 14.3 %collective-permute-start.10 = (bf16[4,32,128]{2,1,0:T(8,128)(2,1)S(1)}, bf16[4,32,128]{2,1,0:T(8,128)(2,1)S(1)}, u32[]{:S(2)}, u32[]{:S(2)}) collective-permute-start(bf16[4,32,128]{2,1,0:T(8,128)(2,1)S(1)} %get-tuple-element.22), channel_id=1, source_target_pairs={{0,1},{1,2},{2,3},{4,5},{5,6},{6,7},{8,9},{9,10},{10,11},{12,13},{... | collective-permute-start | bytes 98312 | tf_op jit(solution)/shard_map/ppermute | solution.py:279
  82.9 1.9 %collective-permute-start.11 = (bf16[4,32,128]{2,1,0:T(8,128)(2,1)S(1)}, bf16[4,32,128]{2,1,0:T(8,128)(2,1)S(1)}, u32[]{:S(2)}, u32[]{:S(2)}) collective-permute-start(bf16[4,32,128]{2,1,0:T(8,128)(2,1)S(1)} %get-tuple-element.21), channel_id=1, source_target_pairs={{1,0},{2,1},{3,2},{5,4},{6,5},{7,6},{9,8},{10,9},{11,10},{13,12},{... | collective-permute-start | bytes 98312 | tf_op jit(solution)/shard_map/ppermute | solution.py:280
  84.8 0.0 copy-done.2
  84.8 0.0 collective-permute-done.10.low_ref
  84.8 3.3 %collective-permute-done.11.high_ref = bf16[4,32,128]{2,1,0:T(8,128)(2,1)S(1)} collective-permute-done((bf16[4,32,128]{2,1,0:T(8,128)(2,1)S(1)}, bf16[4,32,128]{2,1,0:T(8,128)(2,1)S(1)}, u32[]{:S(2)}, u32[]{:S(2)}) %collective-permute-start.11) | collective-permute-done | bytes 32800 | tf_op jit(solution)/shard_map/ppermute | solution.py:280
  88.1 1.4 %detect.1 = f32[128,512]{1,0:T(8,128)} custom-call(f32[1,41]{1,0:T(1,128)S(1)} %bitcast_convert_fusion.taps_ref, bf16[4,128,128]{2,1,0:T(8,128)(2,1)S(1)} %fusion.2.mid_ref, bf16[4,32,128]{2,1,0:T(8,128)(2,1)S(1)} %collective-permute-done.10.low_ref, bf16[4,32,128]{2,1,0:T(8,128)(2,1)S(1)} %collective-permute-done.11.high_ref), custom_call_target="tpu_custom_call" | custom-call | tf_op jit(solution)/shard_map/detect/pallas_call | solution.py:150
  (12 shorter events, 0.2 us)
Async XLA Ops:
  1.4 10.4 %collective-permute-start = (f32[2,32]{1,0:T(2,128)S(1)}, f32[2,32]{1,0:T(2,128)S(1)}, u32[]{:S(2)}, u32[]{:S(2)}) collective-permute-start(f32[2,32]{1,0:T(2,128)S(1)} %pad_maximum_fusion.3), channel_id=1, source_target_pairs={{0,1},{1,0},{2,3},{3,2},{4,5},{5,4},{6,7},{7,6},{8,9},{9,8},{10,11... | collective-permute-start | bytes 776 | tf_op jit(solution)/shard_map/ppermute | solution.py:201
  1.5 10.3 %collective-permute-start.1 = (f32[2,32]{1,0:T(2,128)S(1)}, f32[2,32]{1,0:T(2,128)S(1)}, u32[]{:S(2)}, u32[]{:S(2)}) collective-permute-start(f32[2,32]{1,0:T(2,128)S(1)} %pad_maximum_fusion.3), channel_id=1, source_target_pairs={{0,2},{1,3},{2,0},{3,1},{4,6},{5,7},{6,4},{7,5},{8,10},{9,11},{10,... | collective-permute-start | bytes 776 | tf_op jit(solution)/shard_map/ppermute | solution.py:201
  4.2 7.6 %collective-permute-start.2 = (f32[2,32]{1,0:T(2,128)S(1)}, f32[2,32]{1,0:T(2,128)S(1)}, u32[]{:S(2)}, u32[]{:S(2)}) collective-permute-start(f32[2,32]{1,0:T(2,128)S(1)} %pad_maximum_fusion.3), channel_id=1, source_target_pairs={{0,3},{1,2},{2,1},{3,0},{4,7},{5,6},{6,5},{7,4},{8,11},{9,10},{10,... | collective-permute-start | bytes 776 | tf_op jit(solution)/shard_map/ppermute | solution.py:201
  5.6 1.5 %copy-start = (bf16[168,5376]{1,0:T(8,128)(2,1)S(1)}, bf16[168,5376]{1,0:T(8,128)(2,1)}, u32[]{:S(2)}) copy-start(bf16[168,5376]{1,0:T(8,128)(2,1)} %raw_ref.1) | copy-start | bytes 5419012
  7.1 29.4 %copy-start.1 = (f32[6]{0:T(128)S(1)}, f32[6]{0:T(128)}, u32[]{:S(2)}) copy-start(f32[6]{0:T(128)} %param.18) | copy-start | bytes 76
  11.3 26.1 %collective-permute-start.3 = (bf16[32,128,128]{2,1,0:T(8,128)(2,1)S(1)}, bf16[32,128,128]{2,1,0:T(8,128)(2,1)S(1)}, u32[]{:S(2)}, u32[]{:S(2)}) collective-permute-start(bf16[32,128,128]{2,1,0:T(8,128)(2,1)S(1)} %match_blocks.1.rest_0_), channel_id=1, source_target_pairs={{0,1},{1,0},{2,3},{3,2},{4,5},{5,4},{6,7},{7,6},{8,9},{9,8},{10,11... | collective-permute-start | bytes 3145736 | tf_op jit(solution)/shard_map/ppermute | solution.py:162
  38.9 8.1 %collective-permute-start.4 = (bf16[16,128,128]{2,1,0:T(8,128)(2,1)S(1)}, bf16[16,128,128]{2,1,0:T(8,128)(2,1)S(1)}, u32[]{:S(2)}, u32[]{:S(2)}) collective-permute-start(bf16[16,128,128]{2,1,0:T(8,128)(2,1)S(1)} %get-tuple-element.10), channel_id=1, source_target_pairs={{0,2},{1,3},{2,0},{3,1},{4,6},{5,7},{6,4},{7,5},{8,10},{9,11},{10,... | collective-permute-start | bytes 1572872 | tf_op jit(solution)/shard_map/ppermute | solution.py:162
  40.2 8.2 %collective-permute-start.6 = (bf16[16,128,128]{2,1,0:T(8,128)(2,1)S(1)}, bf16[16,128,128]{2,1,0:T(8,128)(2,1)S(1)}, u32[]{:S(2)}, u32[]{:S(2)}) collective-permute-start(bf16[16,128,128]{2,1,0:T(8,128)(2,1)S(1)} %get-tuple-element.12), channel_id=1, source_target_pairs={{0,4},{4,0},{8,12},{12,8},{16,20},{20,16},{24,28},{28,24},{1,5},{5... | collective-permute-start | bytes 1572872 | tf_op jit(solution)/shard_map/ppermute | solution.py:162
  47.1 8.0 %collective-permute-start.5 = (bf16[8,128,128]{2,1,0:T(8,128)(2,1)S(1)}, bf16[8,128,128]{2,1,0:T(8,128)(2,1)S(1)}, u32[]{:S(2)}, u32[]{:S(2)}) collective-permute-start(bf16[8,128,128]{2,1,0:T(8,128)(2,1)S(1)} %add_convert_fusion.1), channel_id=1, source_target_pairs={{0,4},{4,0},{8,12},{12,8},{16,20},{20,16},{24,28},{28,24},{1,5},{5... | collective-permute-start | bytes 786440 | tf_op jit(solution)/shard_map/ppermute | solution.py:162
  48.5 8.5 %collective-permute-start.7 = (bf16[8,128,128]{2,1,0:T(8,128)(2,1)S(1)}, bf16[8,128,128]{2,1,0:T(8,128)(2,1)S(1)}, u32[]{:S(2)}, u32[]{:S(2)}) collective-permute-start(bf16[8,128,128]{2,1,0:T(8,128)(2,1)S(1)} %add_convert_fusion), channel_id=1, source_target_pairs={{0,2},{1,3},{2,0},{3,1},{4,6},{5,7},{6,4},{7,5},{8,10},{9,11},{10,... | collective-permute-start | bytes 786440 | tf_op jit(solution)/shard_map/ppermute | solution.py:162
  55.1 29.7 %copy-start.2 = (f32[41]{0:T(128)S(1)}, f32[41]{0:T(128)}, u32[]{:S(2)}) copy-start(f32[41]{0:T(128)} %param.19) | copy-start | bytes 496
  57.0 5.6 %collective-permute-start.8 = (bf16[2,4,128,128]{3,2,1,0:T(8,128)(2,1)S(1)}, bf16[2,4,128,128]{3,2,1,0:T(8,128)(2,1)S(1)}, u32[]{:S(2)}, u32[]{:S(2)}) collective-permute-start(bf16[2,4,128,128]{3,2,1,0:T(8,128)(2,1)S(1)} %pad_maximum_fusion), channel_id=1, source_target_pairs={{0,8},{4,12},{8,0},{12,4},{16,24},{20,28},{24,16},{28,20},{1,9},{5... | collective-permute-start | bytes 786440 | tf_op jit(solution)/shard_map/ppermute | solution.py:162
  62.6 5.9 %collective-permute-start.9 = (bf16[1,4,128,128]{3,2,1,0:T(8,128)(2,1)S(1)}, bf16[1,4,128,128]{3,2,1,0:T(8,128)(2,1)S(1)}, u32[]{:S(2)}, u32[]{:S(2)}) collective-permute-start(bf16[1,4,128,128]{3,2,1,0:T(8,128)(2,1)S(1)} %fusion.1), channel_id=1, source_target_pairs={{0,16},{4,20},{8,24},{12,28},{16,0},{20,4},{24,8},{28,12},{1,17},{... | collective-permute-start | bytes 393224 | tf_op jit(solution)/shard_map/ppermute | solution.py:162
  68.6 16.2 %collective-permute-start.10 = (bf16[4,32,128]{2,1,0:T(8,128)(2,1)S(1)}, bf16[4,32,128]{2,1,0:T(8,128)(2,1)S(1)}, u32[]{:S(2)}, u32[]{:S(2)}) collective-permute-start(bf16[4,32,128]{2,1,0:T(8,128)(2,1)S(1)} %get-tuple-element.22), channel_id=1, source_target_pairs={{0,1},{1,2},{2,3},{4,5},{5,6},{6,7},{8,9},{9,10},{10,11},{12,13},{... | collective-permute-start | bytes 98312 | tf_op jit(solution)/shard_map/ppermute | solution.py:279
  82.9 5.2 %collective-permute-start.11 = (bf16[4,32,128]{2,1,0:T(8,128)(2,1)S(1)}, bf16[4,32,128]{2,1,0:T(8,128)(2,1)S(1)}, u32[]{:S(2)}, u32[]{:S(2)}) collective-permute-start(bf16[4,32,128]{2,1,0:T(8,128)(2,1)S(1)} %get-tuple-element.21), channel_id=1, source_target_pairs={{1,0},{2,1},{3,2},{5,4},{6,5},{7,6},{9,8},{10,9},{11,10},{13,12},{... | collective-permute-start | bytes 98312 | tf_op jit(solution)/shard_map/ppermute | solution.py:280
